TPU v7x, 32 devices: a whole 2x2x4 slice. The times are simulated.
32 devices in a mesh: dp: 4 (over y, x), grp: 8 (over z, core).
Axes of the slice: x: 2, y: 2, z: 4, core: 2. Of those that a mesh axis runs over, the one named last changes fastest.
Arguments:
- tokens: bfloat16 [16384, 768], P(('dp', 'grp')), may hold values from -6 to 6
- cotangent: bfloat16 [16384, 768], P(('dp', 'grp')), may hold values from -6 to 6
- span_order: int32 [4, 8], P('dp'), may hold values from 0 to 7, each once within a row
- input_master: float32 [768, 5376], P('grp'), may hold values from -0.20207259 to 0.20207259
- output_master: float32 [3840, 768], P('grp'), may hold values from -0.5484828 to 0.5484828
- vector_master: float32 [13, 768], P(None, 'grp'), may hold values from -1.2 to 2.6
- input_first: float32 [768, 5376], P('grp'), may hold values from -0.875 to 0.875
- output_first: float32 [3840, 768], P('grp'), may hold values from -0.4375 to 0.4375
- vector_first: float32 [13, 768], P(None, 'grp'), may hold values from -0.875 to 0.875
- input_second: float32 [768, 5376], P('grp'), may hold values from 0.0028217214 to 0.14108607
- output_second: float32 [3840, 768], P('grp'), may hold values from 0.0014108607 to 0.04232582
- vector_second: float32 [13, 768], P(None, 'grp'), may hold values from 0.0028217214 to 0.14108607
Outputs:
- result: bfloat16 [16384, 768], P(('dp', 'grp'))
- token_grad: bfloat16 [16384, 768], P(('dp', 'grp'))
- input_grad: float32 [768, 5376], P('grp')
- output_grad: float32 [3840, 768], P('grp')
- vector_grad: float32 [13, 768], P(None, 'grp')
- input_moment: float32 [768, 5376], P('grp')
- output_moment: float32 [3840, 768], P('grp')
- vector_moment: float32 [13, 768], P(None, 'grp')
- input_updated: float32 [768, 5376], P('grp')
- output_updated: float32 [3840, 768], P('grp')
- vector_updated: float32 [13, 768], P(None, 'grp')
- clip_norm: float32 [], replicated
Inputs may be any that keep to these rules, and one draw needn't show every extreme that they name: Each row is a permutation; the device at place g of a group holds span span_order[s, g] of its sequence s.
All inputs are finite; a program needn't handle non-finite values.
Results may differ from a plain program's by a relative error of at most 0.013.
The roundings to bfloat16 on the way count: a program that leaves them out, or rounds other values in their place, can miss the bound.
Values may be sent and summed in bfloat16 or wider, within the bound.
A program may use at most 256 MiB of HBM per device.

v0:
```python
import math

import jax
import jax.numpy as jnp
from jax import lax
from jax.sharding import PartitionSpec as P

HEADS = 12
HEAD = 64
ROT = 16
STEP = 10


NORM_EPS = 1e-05
ADAM_EPS = 1e-08
BETA_ONE = 0.9
BETA_TWO = 0.95
RATE_MATRIX = 0.06
RATE_VECTOR = 0.6
DECAY_MATRIX = 0.1
CLIP_LIMIT = 1000.0
THETA_BASE = 10000.0
MASKED = -1e30
ROOT_HALF = 0.7071067811865476
ROOT_TWOPI = 2.5066282746310002


def gelu_exact(inputs):
    return 0.5 * inputs * (1.0 + jax.scipy.special.erf(inputs * ROOT_HALF))


def gelu_slope(inputs):
    return (
        0.5 * (1.0 + jax.scipy.special.erf(inputs * ROOT_HALF))
        + inputs * jnp.exp(-0.5 * inputs * inputs) / ROOT_TWOPI
    )


def layer_norm(inputs, gain_row, bias_row):
    center = inputs - jnp.mean(inputs, axis=-1, keepdims=True)
    inverse = lax.rsqrt(jnp.mean(center * center, axis=-1, keepdims=True) + NORM_EPS)
    normed = center * inverse
    return (normed * gain_row + bias_row, normed, inverse)


def norm_backward(incoming, normed, inverse, gain_row):
    scaled = incoming * gain_row
    grad_input = inverse * (
        scaled
        - jnp.mean(scaled, axis=-1, keepdims=True)
        - normed * jnp.mean(scaled * normed, axis=-1, keepdims=True)
    )
    return (grad_input, jnp.sum(incoming * normed, axis=0), jnp.sum(incoming, axis=0))


def rotate(heads_in, positions):
    half_rot = ROT // 2
    freq_table = THETA_BASE ** (-2.0 * jnp.arange(half_rot, dtype=jnp.float32) / ROT)
    angles = positions[:, None] * freq_table[None, :]
    cosine = jnp.cos(angles)[:, None, :]
    sine_part = jnp.sin(angles)[:, None, :]
    former = heads_in[..., :half_rot]
    latter = heads_in[..., half_rot:ROT]
    return jnp.concatenate(
        [
            former * cosine - latter * sine_part,
            latter * cosine + former * sine_part,
            heads_in[..., ROT:],
        ],
        axis=-1,
    )


def adam_step(master, gradient, moment_one, moment_two, step_rate, decay_rate):
    first_new = BETA_ONE * moment_one + (1.0 - BETA_ONE) * gradient
    second_new = BETA_TWO * moment_two + (1.0 - BETA_TWO) * gradient * gradient
    first_hat = first_new / (1.0 - BETA_ONE**STEP)
    second_hat = second_new / (1.0 - BETA_TWO**STEP)
    updated = master - step_rate * (
        first_hat / (jnp.sqrt(second_hat) + ADAM_EPS) + decay_rate * master
    )
    return (second_new, updated)


def blockify(matrix, groups, parts):
    row_count, col_count = matrix.shape
    tiles = matrix.reshape(groups, row_count // groups, parts, col_count // parts).transpose(
        2, 0, 1, 3
    )
    return tiles.reshape(parts * row_count, col_count // parts)


def take_piece(matrix, owner, parts, along):
    piece_size = matrix.shape[along] // parts
    return lax.dynamic_slice_in_dim(matrix, owner * piece_size, piece_size, along)


def square_sum(arrays):
    return sum((jnp.sum(member * member) for member in arrays))


def keep_state(state_in):
    return state_in


def body(
    tokens,
    cotangent,
    span_order,
    input_master,
    output_master,
    vector_master,
    input_first,
    output_first,
    vector_first,
    input_second,
    output_second,
    vector_second,
):
    weight_in, weight_out, weight_vec = (
        lax.all_gather(input_master.astype(jnp.bfloat16), "grp", axis=0, tiled=True),
        lax.all_gather(output_master.astype(jnp.bfloat16), "grp", axis=0, tiled=True),
        lax.all_gather(vector_master.astype(jnp.bfloat16), "grp", axis=1, tiled=True),
    )
    width = weight_out.shape[1]
    rows_here = tokens.shape[0]
    groups = lax.axis_size("grp")
    parts = lax.axis_size("dp")
    score_scale = 1.0 / math.sqrt(HEAD)
    vector_rows = weight_vec.astype(jnp.float32)
    inputs = tokens.astype(jnp.float32)
    attn_in, normed_one, inverse_one = layer_norm(inputs, vector_rows[0], vector_rows[1])
    attn_in = attn_in.astype(jnp.bfloat16)
    feed_in, normed_two, inverse_two = layer_norm(inputs, vector_rows[2], vector_rows[3])
    feed_in = feed_in.astype(jnp.bfloat16)
    projected = jnp.dot(
        attn_in, weight_in[:, : 3 * width], preferred_element_type=jnp.float32
    ) + vector_rows[4:7].reshape(-1)
    hidden_pre = jnp.dot(
        feed_in, weight_in[:, 3 * width :], preferred_element_type=jnp.float32
    ) + vector_rows[7:11].reshape(-1)
    order_row = span_order[0]
    group_ids = jnp.arange(groups, dtype=jnp.int32)
    own_span = jnp.sum(jnp.where(group_ids == lax.axis_index("grp"), order_row, 0))
    query_pos = own_span * rows_here + jnp.arange(rows_here, dtype=jnp.int32)
    query_angle = query_pos.astype(jnp.float32)
    queries = rotate(projected[:, :width].reshape(rows_here, HEADS, HEAD), query_angle).astype(
        jnp.bfloat16
    )
    key_rows = (
        rotate(projected[:, width : 2 * width].reshape(rows_here, HEADS, HEAD), query_angle)
        .astype(jnp.bfloat16)
        .reshape(rows_here, width)
    )
    value_rows = projected[:, 2 * width :].astype(jnp.bfloat16)

    def span_positions(piece_rows):
        index = jnp.arange(piece_rows, dtype=jnp.int32)
        owner = index // rows_here
        within = index % rows_here
        chosen = jnp.sum(
            jnp.where(owner[:, None] == group_ids[None, :], order_row[None, :], 0), axis=1
        )
        return chosen * rows_here + within

    start_forward = (
        jnp.zeros((HEADS, rows_here, HEAD), jnp.float32),
        jnp.full((HEADS, rows_here), MASKED, jnp.float32),
        jnp.zeros((HEADS, rows_here), jnp.float32),
    )
    key_all, value_all = (
        lax.all_gather(key_rows, "grp", axis=0, tiled=True),
        lax.all_gather(value_rows, "grp", axis=0, tiled=True),
    )
    running = start_forward
    piece_rows = key_all.shape[0]
    block_rows = math.gcd(piece_rows, 512)
    blocks = piece_rows // block_rows
    key_pos = span_positions(piece_rows).reshape(blocks, block_rows)
    key_blocks = key_all.reshape(blocks, block_rows, HEADS, HEAD)
    value_blocks = value_all.reshape(blocks, block_rows, HEADS, HEAD)

    def attend(state_in, block_item):
        key_block, value_block, positions = block_item
        visible = positions[None, :] <= query_pos[:, None]

        def update(state_now):
            context_sum, row_max, row_total = state_now
            scores = (
                jnp.einsum("qhe,khe->hqk", queries, key_block, preferred_element_type=jnp.float32)
                * score_scale
            )
            scores = jnp.where(visible[None], scores, MASKED)
            new_max = jnp.maximum(row_max, jnp.max(scores, axis=-1))
            weights = jnp.where(visible[None], jnp.exp(scores - new_max[..., None]), 0.0)
            factor = jnp.exp(row_max - new_max)
            context_sum = context_sum * factor[..., None] + jnp.einsum(
                "hqk,khe->hqe",
                weights.astype(jnp.bfloat16),
                value_block,
                preferred_element_type=jnp.float32,
            )
            return (context_sum, new_max, row_total * factor + jnp.sum(weights, axis=-1))

        return (lax.cond(jnp.any(visible), update, keep_state, state_in), None)

    running, _ = lax.scan(attend, running, (key_blocks, value_blocks, key_pos))
    context_sum, row_max, row_total = running
    context_full = (context_sum / row_total[..., None]).transpose(1, 0, 2)
    log_total = row_max + jnp.log(row_total)
    context_low = context_full.reshape(rows_here, width).astype(jnp.bfloat16)
    hidden_act = gelu_exact(hidden_pre).astype(jnp.bfloat16)
    mixed = (
        inputs
        + jnp.dot(context_low, weight_out[:width], preferred_element_type=jnp.float32)
        + jnp.dot(hidden_act, weight_out[width:], preferred_element_type=jnp.float32)
        + vector_rows[11]
        + vector_rows[12]
    )
    result = mixed.astype(jnp.bfloat16)
    contract_rows = (((0,), (0,)), ((), ()))
    grad_context = jnp.dot(
        cotangent, weight_out[:width].T, preferred_element_type=jnp.float32
    ).astype(jnp.bfloat16)
    grad_hidden = (
        jnp.dot(cotangent, weight_out[width:].T, preferred_element_type=jnp.float32)
        * gelu_slope(hidden_pre)
    ).astype(jnp.bfloat16)
    raw_out = jnp.concatenate(
        [
            lax.dot_general(
                context_low, cotangent, contract_rows, preferred_element_type=jnp.float32
            ),
            lax.dot_general(
                hidden_act, cotangent, contract_rows, preferred_element_type=jnp.float32
            ),
        ],
        axis=0,
    )
    grad_heads = grad_context.reshape(rows_here, HEADS, HEAD)
    row_dot = jnp.einsum("qhe,qhe->hq", grad_heads.astype(jnp.float32), context_full)
    start_backward = (
        jnp.zeros((rows_here, HEADS, HEAD), jnp.float32),
        jnp.zeros((groups * rows_here, width), jnp.float32),
        jnp.zeros((groups * rows_here, width), jnp.float32),
    )
    running = start_backward
    piece_rows = key_all.shape[0]
    block_rows = math.gcd(piece_rows, 512)
    blocks = piece_rows // block_rows
    key_pos = span_positions(piece_rows).reshape(blocks, block_rows)
    key_blocks = key_all.reshape(blocks, block_rows, HEADS, HEAD)
    value_blocks = value_all.reshape(blocks, block_rows, HEADS, HEAD)
    offsets = 0 + jnp.arange(blocks, dtype=jnp.int32) * block_rows

    def attend_back(state_in, block_item):
        key_block, value_block, positions, offset = block_item
        visible = positions[None, :] <= query_pos[:, None]

        def update(state_now):
            grad_query, grad_keys, grad_values = state_now
            scores = (
                jnp.einsum("qhe,khe->hqk", queries, key_block, preferred_element_type=jnp.float32)
                * score_scale
            )
            chances = jnp.where(visible[None], jnp.exp(scores - log_total[..., None]), 0.0)
            grad_value = jnp.einsum(
                "hqk,qhe->khe",
                chances.astype(jnp.bfloat16),
                grad_heads,
                preferred_element_type=jnp.float32,
            )
            grad_chance = jnp.einsum(
                "qhe,khe->hqk", grad_heads, value_block, preferred_element_type=jnp.float32
            )
            grad_score = (chances * (grad_chance - row_dot[..., None])).astype(jnp.bfloat16)
            grad_query = (
                grad_query
                + jnp.einsum(
                    "hqk,khe->qhe", grad_score, key_block, preferred_element_type=jnp.float32
                )
                * score_scale
            )
            grad_key = (
                jnp.einsum("hqk,qhe->khe", grad_score, queries, preferred_element_type=jnp.float32)
                * score_scale
            )
            grad_keys = lax.dynamic_update_slice_in_dim(
                grad_keys,
                lax.dynamic_slice_in_dim(grad_keys, offset, block_rows, 0)
                + grad_key.reshape(block_rows, width),
                offset,
                0,
            )
            grad_values = lax.dynamic_update_slice_in_dim(
                grad_values,
                lax.dynamic_slice_in_dim(grad_values, offset, block_rows, 0)
                + grad_value.reshape(block_rows, width),
                offset,
                0,
            )
            return (grad_query, grad_keys, grad_values)

        return (lax.cond(jnp.any(visible), update, keep_state, state_in), None)

    running, _ = lax.scan(attend_back, running, (key_blocks, value_blocks, key_pos, offsets))
    grad_query, grad_keys, grad_values = running
    grad_keys, grad_values = (
        lax.psum_scatter(
            grad_keys.astype(jnp.bfloat16), "grp", scatter_dimension=0, tiled=True
        ).astype(jnp.float32),
        lax.psum_scatter(
            grad_values.astype(jnp.bfloat16), "grp", scatter_dimension=0, tiled=True
        ).astype(jnp.float32),
    )
    grad_proj = jnp.concatenate(
        [
            rotate(grad_query, -query_angle).reshape(rows_here, width),
            rotate(grad_keys.reshape(rows_here, HEADS, HEAD), -query_angle).reshape(
                rows_here, width
            ),
            grad_values,
        ],
        axis=1,
    ).astype(jnp.bfloat16)
    raw_in = jnp.concatenate(
        [
            lax.dot_general(attn_in, grad_proj, contract_rows, preferred_element_type=jnp.float32),
            lax.dot_general(
                feed_in, grad_hidden, contract_rows, preferred_element_type=jnp.float32
            ),
        ],
        axis=1,
    )
    back_one = jnp.dot(grad_proj, weight_in[:, : 3 * width].T, preferred_element_type=jnp.float32)
    back_two = jnp.dot(grad_hidden, weight_in[:, 3 * width :].T, preferred_element_type=jnp.float32)
    input_one, gain_one, bias_one = norm_backward(back_one, normed_one, inverse_one, vector_rows[0])
    input_two, gain_two, bias_two = norm_backward(back_two, normed_two, inverse_two, vector_rows[2])
    token_grad = (cotangent.astype(jnp.float32) + input_one + input_two).astype(jnp.bfloat16)
    out_sum = jnp.sum(cotangent, axis=0, dtype=jnp.float32)
    raw_vec = jnp.concatenate(
        [
            jnp.stack([gain_one, bias_one, gain_two, bias_two]),
            jnp.sum(grad_proj, axis=0, dtype=jnp.float32).reshape(3, width),
            jnp.sum(grad_hidden, axis=0, dtype=jnp.float32).reshape(-1, width),
            jnp.stack([out_sum, out_sum]),
        ],
        axis=0,
    )
    matrix_pieces = (
        lax.psum_scatter(
            blockify(raw_in, groups, parts), ("dp", "grp"), scatter_dimension=0, tiled=True
        ),
        lax.psum_scatter(
            blockify(raw_out, groups, parts), ("dp", "grp"), scatter_dimension=0, tiled=True
        ),
    )
    matrix_total, vector_sum = lax.psum((square_sum(matrix_pieces), raw_vec), ("dp", "grp"))
    total = matrix_total + jnp.sum(vector_sum * vector_sum)
    owner = lax.axis_index("dp")
    pieces = (
        matrix_pieces[0],
        matrix_pieces[1],
        take_piece(vector_sum, lax.axis_index("grp"), groups, 1),
    )
    masters = (
        take_piece(input_master, owner, parts, 1),
        take_piece(output_master, owner, parts, 1),
        vector_master,
    )
    firsts = (
        take_piece(input_first, owner, parts, 1),
        take_piece(output_first, owner, parts, 1),
        vector_first,
    )
    seconds = (
        take_piece(input_second, owner, parts, 1),
        take_piece(output_second, owner, parts, 1),
        vector_second,
    )
    clip_norm = jnp.sqrt(total)
    factor = jnp.minimum(1.0, CLIP_LIMIT / (clip_norm + 1e-06))
    input_grad = factor * pieces[0]
    output_grad = factor * pieces[1]
    vector_grad = factor * pieces[2]
    input_moment, input_updated = adam_step(
        masters[0], input_grad, firsts[0], seconds[0], RATE_MATRIX, DECAY_MATRIX
    )
    output_moment, output_updated = adam_step(
        masters[1], output_grad, firsts[1], seconds[1], RATE_MATRIX, DECAY_MATRIX
    )
    vector_moment, vector_updated = adam_step(
        masters[2], vector_grad, firsts[2], seconds[2], RATE_VECTOR, 0.0
    )
    gathered = (
        lax.all_gather(input_grad.astype(jnp.bfloat16), "dp", axis=1, tiled=True).astype(
            input_grad.dtype
        ),
        lax.all_gather(output_grad.astype(jnp.bfloat16), "dp", axis=1, tiled=True).astype(
            output_grad.dtype
        ),
        lax.all_gather(input_moment.astype(jnp.bfloat16), "dp", axis=1, tiled=True).astype(
            input_moment.dtype
        ),
        lax.all_gather(output_moment.astype(jnp.bfloat16), "dp", axis=1, tiled=True).astype(
            output_moment.dtype
        ),
        lax.all_gather(input_updated.astype(jnp.bfloat16), "dp", axis=1, tiled=True).astype(
            input_updated.dtype
        ),
        lax.all_gather(output_updated.astype(jnp.bfloat16), "dp", axis=1, tiled=True).astype(
            output_updated.dtype
        ),
    )
    input_grad, output_grad, input_moment, output_moment, input_updated, output_updated = gathered
    return (
        result,
        token_grad,
        input_grad,
        output_grad,
        vector_grad,
        input_moment,
        output_moment,
        vector_moment,
        input_updated,
        output_updated,
        vector_updated,
        clip_norm,
    )


def solution(mesh):
    return jax.shard_map(
        body,
        mesh=mesh,
        in_specs=(
            P(("dp", "grp"), None),
            P(("dp", "grp"), None),
            P("dp", None),
            P("grp", None),
            P("grp", None),
            P(None, "grp"),
            P("grp", None),
            P("grp", None),
            P(None, "grp"),
            P("grp", None),
            P("grp", None),
            P(None, "grp"),
        ),
        out_specs=(
            P(("dp", "grp"), None),
            P(("dp", "grp"), None),
            P("grp", None),
            P("grp", None),
            P(None, "grp"),
            P("grp", None),
            P("grp", None),
            P(None, "grp"),
            P("grp", None),
            P("grp", None),
            P(None, "grp"),
            P(),
        ),
        check_vma=False,
    )
```

profile of v0, /device:TPU:0, one launch (start us, length us, event | category | flops | bytes accessed | tf_op | source)
XLA Modules:
  0.0 1500.9 jit_solution(12634044575717769141)
XLA Ops:
  11.2 15.8 %all-gather = bf16[8,96,13]{1,2,0:T(8,128)(2,1)S(1)} all-gather(bf16[1,96,13]{1,2,0:T(8,128)(2,1)S(1)} %convert_bitcast_fusion), channel_id=1, replica_groups=mesh['dp'=4,'grp'=8] {'grp'}, dimensions={0}, use_global_device_ids=true | all-gather | bytes 22464 | tf_op jit(solution)/shard_map/all_gather | solution.py:123
  30.4 63.6 %all-gather.9.cloned.1.call-done = bf16[768,5376]{1,0:T(8,128)(2,1)} async-done(((bf16[96,5376]{1,0:T(8,128)(2,1)}), bf16[768,5376]{1,0:T(8,128)(2,1)}) %all-gather.9.cloned.1.call-update) | async-done | bytes 8257552 | tf_op jit(solution)/shard_map/all_gather | solution.py:121
  110.5 45.8 %all-gather.15.cloned.1.call-done = bf16[3840,768]{1,0:T(8,128)(2,1)} async-done(((bf16[480,768]{1,0:T(8,128)(2,1)}), bf16[3840,768]{1,0:T(8,128)(2,1)}) %all-gather.15.cloned.1.call-update) | async-done | bytes 5898256 | tf_op jit(solution)/shard_map/all_gather | solution.py:122
  159.5 62.4 %all-gather.11.cloned.1.call-done = bf16[4096,768]{0,1:T(8,128)(2,1)} async-done(((bf16[512,768]{0,1:T(8,128)(2,1)}), bf16[4096,768]{0,1:T(8,128)(2,1)}) %all-gather.11.cloned.1.call-update) | async-done | bytes 6291472 | tf_op jit(solution)/shard_map/all_gather | solution.py:172
  221.9 7.0 copy.203
  228.9 5.0 copy.166
  233.8 53.6 %all-gather.13.cloned.1.call-done = bf16[4096,768]{1,0:T(8,128)(2,1)} async-done(((bf16[512,768]{1,0:T(8,128)(2,1)}), bf16[4096,768]{1,0:T(8,128)(2,1)}) %all-gather.13.cloned.1.call-update) | async-done | bytes 6291472 | tf_op jit(solution)/shard_map/all_gather | solution.py:173
  287.5 8.8 copy.165
  296.2 7.0 copy.204
  303.2 5.0 copy.167
  308.4 24.7 %while.30 = (s32[]{:T(128)}, f32[12,512,64]{1,2,0:T(8,128)S(1)}, f32[12,512]{1,0:T(8,128)S(1)}, f32[12,512]{1,0:T(8,128)S(1)}, s32[8,512]{1,0:T(8,128)S(1)}, /*i...) while((s32[]{:T(128)}, f32[12,512,64]{1,2,0:T(8,128)S(1)}, ...), condition=%wide.region_10.11_spmd.clone, body=%wide.region_4.10_spmd.clone.sunk | while | flops 847524352 | bytes 44707048 | solution.py:207
  310.2 11.4 conditional.6
  316.9 4.8 multiply_add_fusion
  335.4 6.1 broadcast.244
  341.5 6.0 broadcast.244.clone
  348.9 62.6 %while.31 = (s32[]{:T(128)}, f32[512,12,64]{0,2,1:T(8,128)}, f32[4096,768]{0,1:T(8,128)}, f32[4096,768]{0,1:T(8,128)}, s32[8,512]{1,0:T(8,128)S(1)}, /*index=5*/...) while((s32[]{:T(128)}, f32[512,12,64]{0,2,1:T(8,128)}, ...), condition=%wide.region_15.16_spmd.clone, body=%wide.region_11.15_spmd.clone.sunk | while | flops 2047214080 | bytes 110186448 | solution.py:306
  351.0 49.2 %conditional.7 = ((f32[512,12,64]{0,2,1:T(8,128)}, f32[4096,768]{0,1:T(8,128)}, f32[4096,768]{0,1:T(8,128)})) conditional(s32[]{:T(128)} %convert_element_type.299, (f32[512,12,64]{0,2,1:T(8,128)}, f32[4096,768]{0,1:T(8,128)}, f32[4096,768]{0,1:T(8,128)}) %tuple.145, (pred[512,512]{0,1:T(8,128)(4,1)S(1)}, ...), branch_computations={%region_13.13_spmd, %region_14.14_spmd.clone} | conditional | flops 2046689280 | bytes 109913776 | solution.py:304
  356.7 5.7 fusion.25
  378.0 8.2 dynamic_update_slice.11
  386.2 8.3 dynamic_update_slice.10
  394.5 5.7 bitcast_add_fusion.2
  411.6 8.2 convert_element_type.151
  419.9 8.2 convert_element_type.152
  429.3 6.8 multiply_convert_fusion
  436.1 5.0 fusion.115
  441.9 8.8 pad_maximum_fusion.1
  450.8 12.5 copy.172
  463.3 15.2 %reshape.264 = f32[8,480,4,192]{1,0,3,2:T(8,128)} reshape(f32[3840,768]{0,1:T(8,128)} %copy.172) | data formatting | bytes 23592960 | tf_op jit(solution)/shard_map/reshape | solution.py:87
  478.5 17.6 %copy.198 = f32[4,8,480,192]{3,2,1,0:T(8,128)} copy(f32[4,8,480,192]{2,1,3,0:T(8,128)} %bitcast.148) | data formatting | bytes 23592960
  497.2 7.9 convert_reduce_fusion
  505.1 5.5 fusion.106
  512.8 396.3 %reduce-scatter.7.cloned.1.call-done = bf16[512,768]{0,1:T(8,128)(2,1)} async-done(((bf16[4096,768]{0,1:T(8,128)(2,1)}), bf16[512,768]{0,1:T(8,128)(2,1)}) %reduce-scatter.7.cloned.1.call-update) | async-done | bytes 786448 | tf_op jit(solution)/shard_map/reduce_scatter | solution.py:309
  913.0 66.5 %reduce-scatter.9.cloned.1.call-done = bf16[512,768]{0,1:T(8,128)(2,1)} async-done(((bf16[4096,768]{0,1:T(8,128)(2,1)}), bf16[512,768]{0,1:T(8,128)(2,1)}) %reduce-scatter.9.cloned.1.call-update) | async-done | bytes 786448 | tf_op jit(solution)/shard_map/reduce_scatter | solution.py:312
  983.4 6.2 pad_maximum_fusion
  989.6 22.2 %reshape.262 = f32[8,96,4,1344]{3,2,1,0:T(4,128)} reshape(f32[768,5376]{1,0:T(8,128)} %pad_maximum_fusion) | data formatting | bytes 33030144 | tf_op jit(solution)/shard_map/reshape | solution.py:87
  1011.8 14.0 copy.171
  1037.1 7.5 fusion.52
  1044.6 6.2 fusion.50
  1053.1 5.7 fusion.81
  1061.0 93.3 %reduce-scatter.13.cloned.1.call-done = f32[480,192]{1,0:T(8,128)} async-done(((f32[15360,192]{1,0:T(8,128)}), f32[480,192]{1,0:T(8,128)}) %reduce-scatter.13.cloned.1.call-update) | async-done | bytes 368656
  1156.3 198.7 %reduce-scatter.11.cloned.1.call-done = f32[96,1344]{1,0:T(8,128)} async-done(((f32[3072,1344]{1,0:T(8,128)}), f32[96,1344]{1,0:T(8,128)}) %reduce-scatter.11.cloned.1.call-update) | async-done | bytes 516112 | tf_op jit(solution)/shard_map/reduce_scatter | solution.py:351
  1361.7 39.7 %all-reduce = (f32[]{:T(128)}, f32[13,768]{1,0:T(8,128)S(1)}) all-reduce(f32[]{:T(128)S(6)} %add.288, f32[13,768]{1,0:T(8,128)S(1)} %concatenate.36), channel_id=1, replica_groups=mesh['dp'=4,'grp'=8] {'dp','grp'}, use_global_device_ids=true, to_apply=%region_26.27 | all-reduce | flops 9985 | bytes 79880 | tf_op jit(solution)/shard_map/psum | solution.py:358
  1403.8 12.7 all_gather.39
  1417.9 11.2 all_gather.41
  1430.5 10.8 all_gather.43
  1444.7 13.0 all-gather.1
  1460.7 12.8 all-gather.2
  1476.4 11.6 all-gather.3
  (266 shorter events, 124.3 us)
Async XLA Ops:
  7.2 3.0 copy-start.12
  7.2 4.0 copy-start.31
  7.2 19.9 %copy-start.39 = (s32[1,8]{1,0:T(1,128)S(1)}, s32[1,8]{1,0:T(1,128)}, u32[]{:S(2)}) copy-start(s32[1,8]{1,0:T(1,128)} %param.22) | copy-start | bytes 100
  7.2 21.9 %copy-start.2 = (bf16[512,768]{1,0:T(8,128)(2,1)S(1)}, bf16[512,768]{1,0:T(8,128)(2,1)}, u32[]{:S(2)}) copy-start(bf16[512,768]{1,0:T(8,128)(2,1)} %param.20) | copy-start | bytes 2359300
  7.2 86.8 %all-gather.9.cloned.1.call-start = ((), (), s32[]{:S(2)}) async-start(), calls=%async_computation.4 | async-start | bytes 9289728 | tf_op jit(solution)/shard_map/all_gather | solution.py:121
  10.1 146.2 %all-gather.15.cloned.1.call-start = ((), (), s32[]{:S(2)}) async-start(), calls=%async_computation.7 | async-start | bytes 6635520 | tf_op jit(solution)/shard_map/all_gather | solution.py:122
  11.1 210.8 %all-gather.11.cloned.1.call-start = ((), (), s32[]{:S(2)}) async-start(), calls=%async_computation.5 | async-start | bytes 7077888 | tf_op jit(solution)/shard_map/all_gather | solution.py:172
  27.1 67.0 %copy-start.21 = (f32[768,13]{0,1:T(8,128)}, f32[768,13]{0,1:T(8,128)S(1)}, u32[]{:S(2)}) copy-start(f32[768,13]{0,1:T(8,128)S(1)} %reshape.276) | copy-start | bytes 119812
  29.1 65.0 %copy-start.33 = (f32[768]{0:T(1024)}, f32[768]{0:T(1024)S(1)}, u32[]{:S(2)}) copy-start(f32[768]{0:T(1024)S(1)} %get-tuple-element.626) | copy-start | bytes 9220
  29.1 65.0 %copy-start.37 = (f32[768]{0:T(1024)}, f32[768]{0:T(1024)S(1)}, u32[]{:S(2)}) copy-start(f32[768]{0:T(1024)S(1)} %get-tuple-element.625) | copy-start | bytes 9220
  29.3 64.8 %copy-start.22 = (f32[512]{0:T(512)}, f32[512]{0:T(512)S(1)}, u32[]{:S(2)}) copy-start(f32[512]{0:T(512)S(1)} %broadcast_multiply_fusion.6) | copy-start | bytes 6148
  29.6 64.4 %copy-start.24 = (f32[512]{0:T(512)}, f32[512]{0:T(512)S(1)}, u32[]{:S(2)}) copy-start(f32[512]{0:T(512)S(1)} %add_rsqrt_fusion) | copy-start | bytes 6148
  98.2 2.2 copy-start.5
  102.1 3.1 copy-start.4
  106.3 50.0 %copy-start.9 = (bf16[512,768]{1,0:T(8,128)(2,1)S(1)}, bf16[512,768]{1,0:T(8,128)(2,1)}, u32[]{:S(2)}) copy-start(bf16[512,768]{1,0:T(8,128)(2,1)} %param.21) | copy-start | bytes 2359300
  107.7 179.8 %all-gather.13.cloned.1.call-start = ((), (), s32[]{:S(2)}) async-start(), calls=%async_computation.6 | async-start | bytes 7077888 | tf_op jit(solution)/shard_map/all_gather | solution.py:173
  110.1 799.0 %reduce-scatter.7.cloned.1.call-start = ((), (), s32[]{:S(2)}) async-start(), calls=%async_computation.8 | async-start | bytes 7077888 | tf_op jit(solution)/shard_map/reduce_scatter | solution.py:309
  362.5 2.7 copy-start
  419.8 559.6 %reduce-scatter.9.cloned.1.call-start = ((), (), s32[]{:S(2)}) async-start(), calls=%async_computation.9 | async-start | bytes 7077888 | tf_op jit(solution)/shard_map/reduce_scatter | solution.py:312
  428.1 1.2 copy-start.3
  428.1 1.2 copy-start.19
  428.1 1.2 copy-start.20
  428.1 1.2 copy-start.23
  428.2 726.2 %reduce-scatter.13.cloned.1.call-start = ((), (), s32[]{:S(2)}) async-start(), calls=%async_computation.11 | async-start | bytes 16220160
  429.3 6.8 copy-start.10
  436.1 5.0 copy-start.40
  436.1 5.0 copy-start.7
  496.1 858.9 %reduce-scatter.11.cloned.1.call-start = ((), (), s32[]{:S(2)}) async-start(), calls=%async_computation.10 | async-start | bytes 17842176 | tf_op jit(solution)/shard_map/reduce_scatter | solution.py:351
  505.1 5.5 copy-start.6
  510.7 401.0 %copy-start.27 = (f32[512,8]{0,1:T(8,128)S(1)}, f32[512,8]{0,1:T(8,128)}, u32[]{:S(2)}) copy-start(f32[512,8]{0,1:T(8,128)} %get-tuple-element.708) | copy-start | bytes 49156
  510.7 401.0 %copy-start.28 = (f32[512,8]{0,1:T(8,128)S(1)}, f32[512,8]{0,1:T(8,128)}, u32[]{:S(2)}) copy-start(f32[512,8]{0,1:T(8,128)} %get-tuple-element.709) | copy-start | bytes 49156
  909.1 3.7 copy-start.13
  910.5 69.0 %copy-start.34 = (f32[768]{0:T(1024)S(1)}, f32[768]{0:T(1024)}, u32[]{:S(2)}) copy-start(f32[768]{0:T(1024)} %copy-done.33) | copy-start | bytes 9220
  910.5 69.0 %copy-start.38 = (f32[768]{0:T(1024)S(1)}, f32[768]{0:T(1024)}, u32[]{:S(2)}) copy-start(f32[768]{0:T(1024)} %copy-done.37) | copy-start | bytes 9220
  979.5 3.9 copy-start.1
  1037.1 7.5 copy-start.41
  1044.6 6.2 copy-start.18
  1053.0 5.8 copy-start.17
  1058.8 2.1 copy-start.29
  1058.8 2.1 copy-start.30
  1058.8 299.3 %copy-start.8 = (bf16[512,12,64]{0,2,1:T(8,128)(2,1)S(1)}, bf16[512,12,64]{0,2,1:T(8,128)(2,1)}, u32[]{:S(2)}) copy-start(bf16[512,12,64]{0,2,1:T(8,128)(2,1)} %get-tuple-element.693) | copy-start | bytes 2359300
  1358.1 45.3 %copy-start.15 = (f32[480,192]{0,1:T(8,128)S(1)}, f32[480,192]{0,1:T(8,128)}, u32[]{:S(2)}) copy-start(f32[480,192]{0,1:T(8,128)} %copy.202) | copy-start | bytes 1105924
  1358.1 45.3 %copy-start.16 = (f32[480,192]{0,1:T(8,128)S(1)}, f32[480,192]{0,1:T(8,128)}, u32[]{:S(2)}) copy-start(f32[480,192]{0,1:T(8,128)} %copy.201) | copy-start | bytes 1105924
  1401.4 2.0 copy-start.26
  1417.9 24.8 %copy-start.14 = (f32[96,1344]{1,0:T(8,128)S(1)}, f32[96,1344]{1,0:T(8,128)}, u32[]{:S(2)}) copy-start(f32[96,1344]{1,0:T(8,128)} %reduce-scatter.11.cloned.1.call-done) | copy-start | bytes 1548292
  1488.1 2.9 copy-start.32
  1488.1 2.9 copy-start.35
  1488.1 2.9 copy-start.36
  (2 other events, 2.3 us)
Sparse Core Ops, SparseCore 0:
  10.3 83.7 all-gather.8
  96.2 60.0 all-gather.14
  158.5 63.3 all-gather.10
  224.0 63.4 all-gather.12
  419.9 489.1 reduce-scatter.6
  911.3 68.1 reduce-scatter.8
  985.5 168.8 reduce-scatter.12
  1160.8 194.1 reduce-scatter.10
where the time goes:
time: 1510 us; the launch traced here: 1500 us
  waiting for transfers between devices  980 us (65%)
  local copies, waits for them, and re-layouts  192 us (13%)
  blocking collectives  128 us (8%)
  matrix products  90.5 us (6%)
  other arithmetic  76.4 us (5%)
  between operations  19.8 us (1%)
    reduce_scatter x1, waiting for transfers between devices, body(): lax.psum_scatter(grad_keys.astype(jnp.bfloat16), 'grp', scatter_dimension...  396 us
    reduce_scatter x1, waiting for transfers between devices, body(): lax.psum_scatter(blockify(raw_in, groups, parts), ('dp', 'grp'), scatter_...  199 us
    unnamed x9, waiting for transfers between devices  93.5 us
    reduce_scatter x1, waiting for transfers between devices, body(): lax.psum_scatter(grad_values.astype(jnp.bfloat16), 'grp', scatter_dimensi...  66.5 us
    all_gather x1, waiting for transfers between devices, body(): lax.all_gather(input_master.astype(jnp.bfloat16), 'grp', axis=0, tiled=True)  63.6 us
    all_gather x1, waiting for transfers between devices, body(): lax.all_gather(key_rows, 'grp', axis=0, tiled=True)  62.4 us
    unnamed x94, local copies, waits for them, and re-layouts  55.7 us
    all_gather x1, waiting for transfers between devices, body(): lax.all_gather(value_rows, 'grp', axis=0, tiled=True)  53.6 us
  transfers between devices with their start and end apart: 8, of which 8 were waited for; matrix products, arithmetic and copies ran while one was open for 14% of the time, Pallas kernels for 0%

commit v1 on v0

v1 whole, which is shorter than its diff:
```python
import math

import jax
import jax.numpy as jnp
from jax import lax
from jax.experimental import pallas as pl
from jax.experimental.pallas import tpu as pltpu
from jax.sharding import PartitionSpec as P

HEADS = 12
HEAD = 64
ROT = 16
STEP = 10


NORM_EPS = 1e-05
ADAM_EPS = 1e-08
BETA_ONE = 0.9
BETA_TWO = 0.95
RATE_MATRIX = 0.06
RATE_VECTOR = 0.6
DECAY_MATRIX = 0.1
CLIP_LIMIT = 1000.0
THETA_BASE = 10000.0
MASKED = -1e30
ROOT_HALF = 0.7071067811865476
ROOT_TWOPI = 2.5066282746310002


def gelu_exact(inputs):
    return 0.5 * inputs * (1.0 + jax.scipy.special.erf(inputs * ROOT_HALF))


def gelu_slope(inputs):
    return (
        0.5 * (1.0 + jax.scipy.special.erf(inputs * ROOT_HALF))
        + inputs * jnp.exp(-0.5 * inputs * inputs) / ROOT_TWOPI
    )


def layer_norm(inputs, gain_row, bias_row):
    center = inputs - jnp.mean(inputs, axis=-1, keepdims=True)
    inverse = lax.rsqrt(jnp.mean(center * center, axis=-1, keepdims=True) + NORM_EPS)
    normed = center * inverse
    return (normed * gain_row + bias_row, normed, inverse)


def norm_backward(incoming, normed, inverse, gain_row):
    scaled = incoming * gain_row
    grad_input = inverse * (
        scaled
        - jnp.mean(scaled, axis=-1, keepdims=True)
        - normed * jnp.mean(scaled * normed, axis=-1, keepdims=True)
    )
    return (grad_input, jnp.sum(incoming * normed, axis=0), jnp.sum(incoming, axis=0))


def rotate(heads_in, cosine, sine_part):
    half_rot = ROT // 2
    former = heads_in[:, :half_rot]
    latter = heads_in[:, half_rot:ROT]
    return jnp.concatenate(
        [
            former * cosine - latter * sine_part,
            latter * cosine + former * sine_part,
            heads_in[:, ROT:],
        ],
        axis=1,
    )


def adam_step(master, gradient, moment_one, moment_two, step_rate, decay_rate):
    first_new = BETA_ONE * moment_one + (1.0 - BETA_ONE) * gradient
    second_new = BETA_TWO * moment_two + (1.0 - BETA_TWO) * gradient * gradient
    first_hat = first_new / (1.0 - BETA_ONE**STEP)
    second_hat = second_new / (1.0 - BETA_TWO**STEP)
    updated = master - step_rate * (
        first_hat / (jnp.sqrt(second_hat) + ADAM_EPS) + decay_rate * master
    )
    return (second_new, updated)


def split_alone(heads):
    count, size, rows = heads.shape
    return heads.reshape(count // 3, 3, size, rows)[:, 0::2].reshape(-1, size, rows)


def split_both(heads):
    count, size, rows = heads.shape
    shared = heads.reshape(count // 3, 3, size, rows)[:, 1:2]
    return jnp.broadcast_to(shared, (count // 3, 2, size, rows)).reshape(-1, size, rows)


def fold_half(halves):
    size = halves.shape[1] // 2
    return jnp.concatenate([halves[:, :size], halves[:, size:]], axis=2)


def split_halves(heads):
    count, size, rows = heads.shape
    shared = heads.reshape(count // 3, 3, size, 2, rows // 2)[:, 1]
    return fold_half(shared.transpose(0, 2, 1, 3).reshape(-1, size, rows // 2))


def join_heads(alone, shared):
    devices, size, rows = alone.shape
    pairs = alone.reshape(devices // 2, 2, size, rows)
    return jnp.stack([pairs[:, 0], shared, pairs[:, 1]], axis=1).reshape(-1, size, rows)


def join_halves(packed):
    devices, size, rows = packed.shape
    halves = jnp.concatenate([packed[:, :, : rows // 2], packed[:, :, rows // 2 :]], axis=1)
    halves = halves.reshape(devices // 2, 2, 2 * size, rows // 2).transpose(0, 2, 1, 3)
    return halves.reshape(devices // 2, 2 * size, rows)


def join_both(packed):
    devices, size, rows = packed.shape
    return jnp.sum(packed.astype(jnp.float32).reshape(devices // 2, 2, size, rows), axis=1)


Q_BOTH = HEAD
K_AT = HEAD + HEAD // 2
V_AT = K_AT + 2 * HEAD
PACKED = V_AT + 2 * HEAD


def flip(tile):
    return tile.astype(jnp.float32).T


def take_queries(ref, place, slot):
    if slot == 0:
        return ref[place, :HEAD, :]
    folded = ref[place, Q_BOTH:K_AT, :]
    half = folded.shape[1] // 2
    return jnp.concatenate([folded[:, :half], folded[:, half:]], axis=0)


def visible_mask(keys, count, slot, half):
    key_at = lax.broadcasted_iota(jnp.int32, (keys, count), 0)
    query_at = lax.broadcasted_iota(jnp.int32, (keys, count), 1)
    if slot == 1:
        query_at = query_at + half * count
    return key_at <= query_at


def forward_kernel(span, place_of, half, x_ref, alone_ref, both_ref, la_ref, lb_ref, keys):
    places, _, rows = x_ref.shape

    def stage(place, _):
        for slot in range(2):
            at = K_AT + slot * HEAD
            keys[slot, place] = flip(x_ref[place, at : at + HEAD, :]).astype(jnp.bfloat16)
        return 0

    lax.fori_loop(0, places, stage, 0)
    for slot, (ctx_ref, log_ref) in enumerate(((alone_ref, la_ref), (both_ref, lb_ref))):
        count = ctx_ref.shape[2]
        value_at = V_AT + slot * HEAD

        def work(place, _):
            queries = take_queries(x_ref, place, slot)

            def scores_of(other):
                return jnp.dot(keys[slot, other], queries, preferred_element_type=jnp.float32)

            def weigh(other, weights):
                return jnp.dot(
                    x_ref[other, value_at : value_at + HEAD, :],
                    weights.astype(jnp.bfloat16),
                    preferred_element_type=jnp.float32,
                )

            scores = scores_of(place)
            scores = jnp.where(visible_mask(rows, count, slot, half[0]), scores, MASKED)
            top = jnp.max(scores, axis=0, keepdims=True)
            weights = jnp.exp(scores - top)
            total = jnp.sum(weights, axis=0, keepdims=True)

            def step(index, state):
                context, top, total = state
                other = place_of[index]
                scores = scores_of(other)
                new_top = jnp.maximum(top, jnp.max(scores, axis=0, keepdims=True))
                weights = jnp.exp(scores - new_top)
                factor = jnp.exp(top - new_top)
                total = total * factor + jnp.sum(weights, axis=0, keepdims=True)
                return (context * factor + weigh(other, weights), new_top, total)

            context, top, total = lax.fori_loop(
                0, span[place], step, (weigh(place, weights), top, total)
            )
            ctx_ref[place] = context / total
            log_ref[place] = top + jnp.log(total)
            return 0

        lax.fori_loop(0, places, work, 0)


def backward_kernel(
    span, place_of, half, x_ref, g_ref, alone_ref, both_ref, la_ref, lb_ref,
    out_ref, keys, values, grad_keys, grad_values,
):
    places, _, rows = x_ref.shape

    def stage(place, _):
        for slot in range(2):
            at = K_AT + slot * HEAD
            keys[slot, place] = flip(x_ref[place, at : at + HEAD, :]).astype(jnp.bfloat16)
            at = V_AT + slot * HEAD
            values[slot, place] = flip(x_ref[place, at : at + HEAD, :]).astype(jnp.bfloat16)
            grad_keys[slot, place] = jnp.zeros((rows, HEAD), jnp.float32)
            grad_values[slot, place] = jnp.zeros((rows, HEAD), jnp.float32)
        return 0

    lax.fori_loop(0, places, stage, 0)
    for slot, (ctx_ref, log_ref) in enumerate(((alone_ref, la_ref), (both_ref, lb_ref))):
        count = ctx_ref.shape[2]
        key_at = K_AT + slot * HEAD

        def work(place, _):
            queries = take_queries(x_ref, place, slot)
            grads = take_queries(g_ref, place, slot)
            queries_flat = flip(queries).astype(jnp.bfloat16)
            grads_flat = flip(grads).astype(jnp.bfloat16)
            log_total = log_ref[place]
            row_dot = jnp.sum(grads.astype(jnp.float32) * ctx_ref[place], axis=0, keepdims=True)

            def block(other, masked):
                scores = jnp.dot(keys[slot, other], queries, preferred_element_type=jnp.float32)
                if masked:
                    scores = jnp.where(visible_mask(rows, count, slot, half[0]), scores, MASKED)
                chances = jnp.exp(scores - log_total)
                grad_values[slot, other] += jnp.dot(
                    chances.astype(jnp.bfloat16), grads_flat, preferred_element_type=jnp.float32
                )
                grad_chance = jnp.dot(
                    values[slot, other], grads, preferred_element_type=jnp.float32
                )
                grad_score = (chances * (grad_chance - row_dot)).astype(jnp.bfloat16)
                grad_keys[slot, other] += jnp.dot(
                    grad_score, queries_flat, preferred_element_type=jnp.float32
                )
                return jnp.dot(
                    x_ref[other, key_at : key_at + HEAD, :],
                    grad_score,
                    preferred_element_type=jnp.float32,
                )

            grad_query = lax.fori_loop(
                0,
                span[place],
                lambda index, state: state + block(place_of[index], False),
                block(place, True),
            )
            grad_query = (grad_query * (1.0 / math.sqrt(HEAD))).astype(out_ref.dtype)
            if slot == 0:
                out_ref[place, :HEAD, :] = grad_query
            else:
                out_ref[place, Q_BOTH:K_AT, :] = jnp.concatenate(
                    [grad_query[: HEAD // 2], grad_query[HEAD // 2 :]], axis=1
                )
            return 0

        lax.fori_loop(0, places, work, 0)

    def finish(place, _):
        for slot in range(2):
            at = K_AT + slot * HEAD
            out_ref[place, at : at + HEAD, :] = grad_keys[slot, place].T.astype(out_ref.dtype)
            at = V_AT + slot * HEAD
            out_ref[place, at : at + HEAD, :] = grad_values[slot, place].T.astype(out_ref.dtype)
        return 0

    lax.fori_loop(0, places, finish, 0)


def exchange(packed):
    return lax.all_to_all(packed, "grp", 0, 0, tiled=True)


def local_call(kernel, outputs, scratch, flops, touched, *operands):
    smem = pl.BlockSpec(memory_space=pltpu.SMEM)
    vmem = pl.BlockSpec(memory_space=pltpu.VMEM)
    return pl.pallas_call(
        kernel,
        out_shape=outputs,
        in_specs=[smem] * 3 + [vmem] * (len(operands) - 3),
        out_specs=jax.tree.map(lambda _: vmem, outputs),
        scratch_shapes=scratch,
        compiler_params=pltpu.CompilerParams(vmem_limit_bytes=48 * 1024 * 1024),
        cost_estimate=pl.CostEstimate(
            flops=flops, bytes_accessed=touched, transcendentals=flops // 256
        ),
    )(*operands)


def take_piece(matrix, owner, parts, along):
    piece_size = matrix.shape[along] // parts
    return lax.dynamic_slice_in_dim(matrix, owner * piece_size, piece_size, along)


def square_sum(arrays):
    return sum((jnp.sum(member * member) for member in arrays))


def body(
    tokens,
    cotangent,
    span_order,
    input_master,
    output_master,
    vector_master,
    input_first,
    output_first,
    vector_first,
    input_second,
    output_second,
    vector_second,
):
    width = tokens.shape[1]
    rows_here = tokens.shape[0]
    groups = lax.axis_size("grp")
    score_scale = 1.0 / math.sqrt(HEAD)
    contract_rows = (((0,), (0,)), ((), ()))
    contract_last = (((1,), (1,)), ((), ()))
    flat = (((0,), (1,)), ((), ()))
    f32, bf16 = jnp.float32, jnp.bfloat16

    def gather_rows(shard):
        return lax.all_gather(shard.astype(bf16), "grp", axis=0, tiled=True)

    weight_vec = lax.all_gather(vector_master.astype(bf16), "grp", axis=1, tiled=True)
    weight_attn = gather_rows(input_master[:, : 3 * width])
    weight_ctx = gather_rows(output_master)
    weight_feed = gather_rows(input_master[:, 3 * width :])
    weight_ctx, weight_ffn = weight_ctx[:width], weight_ctx[width:]
    vector_rows = weight_vec.astype(f32)
    inputs = tokens.astype(f32)
    attn_in, normed_one, inverse_one = layer_norm(inputs, vector_rows[0], vector_rows[1])
    attn_in = attn_in.astype(bf16)
    feed_in, normed_two, inverse_two = layer_norm(inputs, vector_rows[2], vector_rows[3])
    feed_in = feed_in.astype(bf16)
    projected = (
        lax.dot_general(weight_attn, attn_in, flat, preferred_element_type=f32)
        + vector_rows[4:7].reshape(-1)[:, None]
    ).reshape(3, HEADS, HEAD, rows_here)
    order_row = span_order[0]
    group_ids = jnp.arange(groups, dtype=jnp.int32)
    place = lax.axis_index("grp")
    own_span = jnp.sum(jnp.where(group_ids == place, order_row, 0))
    place_of = jnp.sum(
        jnp.where(order_row[None, :] == group_ids[:, None], group_ids[None, :], 0), axis=1
    ).astype(jnp.int32)
    half = (place % 2).astype(jnp.int32).reshape(1)
    query_pos = (own_span * rows_here + jnp.arange(rows_here, dtype=jnp.int32)).astype(f32)
    half_rot = ROT // 2
    freq_table = THETA_BASE ** (-2.0 * jnp.arange(half_rot, dtype=f32) / ROT)
    angles = query_pos[None, :] * freq_table[:, None]
    cosine, sine_part = lax.optimization_barrier((jnp.cos(angles), jnp.sin(angles)))
    queries = (rotate(projected[0], cosine, sine_part).astype(bf16) * score_scale).astype(bf16)
    key_heads = rotate(projected[1], cosine, sine_part).astype(bf16)
    value_heads = projected[2].astype(bf16)
    packed = exchange(
        jnp.concatenate(
            [
                split_alone(queries),
                split_halves(queries),
                split_alone(key_heads),
                split_both(key_heads),
                split_alone(value_heads),
                split_both(value_heads),
            ],
            axis=1,
        )
    )
    grad_context = (
        lax.dot_general(weight_ctx, cotangent, contract_last, preferred_element_type=f32)
        .astype(bf16)
        .reshape(HEADS, HEAD, rows_here)
    )
    grad_packed = exchange(
        jnp.concatenate([split_alone(grad_context), split_halves(grad_context)], axis=1)
    )
    tasks = (order_row, place_of, half)
    pair_work = groups * (groups + 1) * 3 * rows_here * rows_here * HEAD
    stage = (2, groups, rows_here, HEAD)
    context_alone, context_both, log_alone, log_both = local_call(
        forward_kernel,
        (
            jax.ShapeDtypeStruct((groups, HEAD, rows_here), f32),
            jax.ShapeDtypeStruct((groups, HEAD, rows_here // 2), f32),
            jax.ShapeDtypeStruct((groups, 1, rows_here), f32),
            jax.ShapeDtypeStruct((groups, 1, rows_here // 2), f32),
        ),
        [pltpu.VMEM(stage, bf16)],
        pair_work * 4,
        packed.size * 4,
        *tasks,
        packed,
    )
    context_back = exchange(
        jnp.concatenate([context_alone, fold_half(context_both)], axis=1).astype(bf16)
    )
    hidden_pre = (
        lax.dot_general(
            feed_in, weight_feed, (((1,), (0,)), ((), ())), preferred_element_type=f32
        )
        + vector_rows[7:11].reshape(-1)
    )
    hidden_act = gelu_exact(hidden_pre).astype(bf16)
    grad_hidden = (
        lax.dot_general(cotangent, weight_ffn, contract_last, preferred_element_type=f32)
        * gelu_slope(hidden_pre)
    ).astype(bf16)

    def scatter_rows(raw):
        return lax.psum_scatter(raw, "grp", scatter_dimension=0, tiled=True)

    def rows_product(left, right):
        return lax.dot_general(left, right, contract_rows, preferred_element_type=f32)

    context_low = join_heads(
        context_back[:, :HEAD], join_halves(context_back[:, HEAD:])
    ).reshape(width, rows_here)
    raw_feed = rows_product(feed_in, grad_hidden).astype(bf16)
    raw_out = jnp.concatenate(
        [
            jnp.dot(context_low, cotangent, preferred_element_type=f32).astype(bf16),
            rows_product(hidden_act, cotangent).astype(bf16),
        ],
        axis=0,
    )
    raw_feed, raw_out, packed, grad_packed = lax.optimization_barrier(
        (raw_feed, raw_out, packed, grad_packed)
    )
    mine_feed, mine_out = scatter_rows(raw_feed), scatter_rows(raw_out)
    sum_feed, sum_out = lax.psum((mine_feed, mine_out), "dp")
    grads_back = exchange(
        local_call(
            backward_kernel,
            jax.ShapeDtypeStruct(packed.shape, bf16),
            [
                pltpu.VMEM(stage, bf16),
                pltpu.VMEM(stage, bf16),
                pltpu.VMEM(stage, f32),
                pltpu.VMEM(stage, f32),
            ],
            pair_work * 10,
            packed.size * 6,
            *tasks,
            packed,
            grad_packed,
            context_alone,
            context_both,
            log_alone,
            log_both,
        )
    )
    result = (
        inputs
        + rows_product(context_low, weight_ctx)
        + jnp.dot(hidden_act, weight_ffn, preferred_element_type=f32)
        + vector_rows[11]
        + vector_rows[12]
    ).astype(bf16)
    back_two = lax.dot_general(
        grad_hidden, weight_feed, contract_last, preferred_element_type=f32
    )
    input_two, gain_two, bias_two = norm_backward(back_two, normed_two, inverse_two, vector_rows[2])
    grad_query = join_heads(
        grads_back[:, :HEAD], join_halves(grads_back[:, Q_BOTH:K_AT])
    ).astype(f32)
    grad_key = join_heads(
        grads_back[:, K_AT : K_AT + HEAD].astype(f32),
        join_both(grads_back[:, K_AT + HEAD : V_AT]),
    )
    grad_value = join_heads(
        grads_back[:, V_AT : V_AT + HEAD].astype(f32),
        join_both(grads_back[:, V_AT + HEAD :]),
    )
    grad_proj = (
        jnp.concatenate(
            [
                rotate(grad_query, cosine, -sine_part),
                rotate(grad_key, cosine, -sine_part),
                grad_value,
            ],
            axis=0,
        )
        .astype(bf16)
        .reshape(3 * width, rows_here)
    )
    raw_attn = lax.dot_general(attn_in, grad_proj, flat, preferred_element_type=f32)
    mine_attn = scatter_rows(raw_attn.astype(bf16))
    mine_attn, sum_feed, sum_out = lax.optimization_barrier((mine_attn, sum_feed, sum_out))
    sum_attn = lax.psum(mine_attn, "dp").astype(f32)
    sum_feed, sum_out = sum_feed.astype(f32), sum_out.astype(f32)
    back_one = lax.dot_general(grad_proj, weight_attn, flat, preferred_element_type=f32)
    input_one, gain_one, bias_one = norm_backward(back_one, normed_one, inverse_one, vector_rows[0])
    token_grad = (cotangent.astype(f32) + input_one + input_two).astype(bf16)
    out_sum = jnp.sum(cotangent, axis=0, dtype=f32)
    raw_vec = jnp.concatenate(
        [
            jnp.stack([gain_one, bias_one, gain_two, bias_two]),
            jnp.sum(grad_proj, axis=1, dtype=f32).reshape(3, width),
            jnp.sum(grad_hidden, axis=0, dtype=f32).reshape(-1, width),
            jnp.stack([out_sum, out_sum]),
        ],
        axis=0,
    )
    vector_sum = lax.psum(raw_vec, ("dp", "grp"))
    matrix_total = lax.psum(square_sum((sum_attn, sum_feed, sum_out)), "grp")
    total = matrix_total + jnp.sum(vector_sum * vector_sum)
    clip_norm = jnp.sqrt(total)
    factor = jnp.minimum(1.0, CLIP_LIMIT / (clip_norm + 1e-06))
    input_grad = factor * jnp.concatenate([sum_attn, sum_feed], axis=1)
    output_grad = factor * sum_out
    vector_grad = factor * take_piece(vector_sum, place, groups, 1)
    input_moment, input_updated = adam_step(
        input_master, input_grad, input_first, input_second, RATE_MATRIX, DECAY_MATRIX
    )
    output_moment, output_updated = adam_step(
        output_master, output_grad, output_first, output_second, RATE_MATRIX, DECAY_MATRIX
    )
    vector_moment, vector_updated = adam_step(
        vector_master, vector_grad, vector_first, vector_second, RATE_VECTOR, 0.0
    )
    return (
        result,
        token_grad,
        input_grad,
        output_grad,
        vector_grad,
        input_moment,
        output_moment,
        vector_moment,
        input_updated,
        output_updated,
        vector_updated,
        clip_norm,
    )


def solution(mesh):
    return jax.shard_map(
        body,
        mesh=mesh,
        in_specs=(
            P(("dp", "grp"), None),
            P(("dp", "grp"), None),
            P("dp", None),
            P("grp", None),
            P("grp", None),
            P(None, "grp"),
            P("grp", None),
            P("grp", None),
            P(None, "grp"),
            P("grp", None),
            P("grp", None),
            P(None, "grp"),
        ),
        out_specs=(
            P(("dp", "grp"), None),
            P(("dp", "grp"), None),
            P("grp", None),
            P("grp", None),
            P(None, "grp"),
            P("grp", None),
            P("grp", None),
            P(None, "grp"),
            P("grp", None),
            P("grp", None),
            P(None, "grp"),
            P(),
        ),
        check_vma=False,
    )
```

time: 1510 us -> 697 us (0.46)
  waiting for transfers between devices: 980 us -> 363 us
  local copies, waits for them, and re-layouts: 192 us -> 32.8 us
  Pallas kernels: 0 us -> 95.4 us
  blocking collectives: 128 us -> 72.4 us
  other arithmetic: 76.4 us -> 33.7 us
  matrix products: 90.5 us -> 56.7 us
    reduce_scatter x3, waiting for transfers between devices: 661 us -> 28.5 us  [scatter_rows(): return lax.psum_scatter(raw, 'grp', scatter_dimension=0, tiled=True)]
    all_to_all x0 -> x4, waiting for transfers between devices: none -> 129 us  [exchange(): return lax.all_to_all(packed, 'grp', 0, 0, tiled=True)]
    pallas_call x0 -> x2, Pallas kernels: none -> 95.4 us  [local_call(): pl.pallas_call(kernel, out_shape=outputs, in_specs=[smem] * 3 + [vmem] *...]
    unnamed x9 -> x8, waiting for transfers between devices: 93.5 us -> 0.65 us
    all_gather x4 -> x3, waiting for transfers between devices: 225 us -> 145 us  [gather_rows(): return lax.all_gather(shard.astype(bf16), 'grp', axis=0, tiled=True)]
    all_gather x7 -> x1, blocking collectives: 87.9 us -> 15.7 us  [body(): lax.all_gather(vector_master.astype(bf16), 'grp', axis=1, tiled=True)]
    psum x0 -> x2, waiting for transfers between devices: none -> 60.8 us  [the longest x1 58.9 us: body(): sum_feed, sum_out = lax.psum((mine_feed, mine_out), 'dp')]
    unnamed x94 -> x85, local copies, waits for them, and re-layouts: 55.7 us -> 10.1 us
  transfers between devices with their start and end apart: 8 -> 12, of which waited for: 8 -> 9; matrix products, arithmetic and copies ran while one was open for 14% -> 15% of each run, Pallas kernels for 0% -> 8%
where the time goes in v1:
time: 697 us; the launch traced here: 691 us
  waiting for transfers between devices  363 us (52%)
  Pallas kernels  95.4 us (14%)
  blocking collectives  72.4 us (10%)
  matrix products  56.7 us (8%)
  other arithmetic  33.7 us (5%)
  local copies, waits for them, and re-layouts  32.8 us (5%)
  between operations  20.7 us (3%)
  starting transfers between devices  15.5 us (2%)
    all_gather x3, waiting for transfers between devices, gather_rows(): return lax.all_gather(shard.astype(bf16), 'grp', axis=0, tiled=True)  145 us
    all_to_all x4, waiting for transfers between devices, exchange(): return lax.all_to_all(packed, 'grp', 0, 0, tiled=True)  129 us
    pallas_call x2, Pallas kernels, local_call(): pl.pallas_call(kernel, out_shape=outputs, in_specs=[smem] * 3 + [vmem] *...  95.4 us
    psum x1, waiting for transfers between devices, body(): sum_feed, sum_out = lax.psum((mine_feed, mine_out), 'dp')  58.9 us
    psum x1, blocking collectives, body(): vector_sum = lax.psum(raw_vec, ('dp', 'grp'))  39.9 us
    reduce_scatter x3, waiting for transfers between devices, scatter_rows(): return lax.psum_scatter(raw, 'grp', scatter_dimension=0, tiled=True)  28.5 us
    psum x1, blocking collectives, body(): matrix_total = lax.psum(square_sum((sum_attn, sum_feed, sum_out)), 'grp')  16.8 us
    all_gather x1, blocking collectives, body(): lax.all_gather(vector_master.astype(bf16), 'grp', axis=1, tiled=True)  15.7 us
  transfers between devices with their start and end apart: 12, of which 9 were waited for; matrix products, arithmetic and copies ran while one was open for 15% of the time, Pallas kernels for 8%

profile of v1, /device:TPU:0, one launch (start us, length us, event | category | flops | bytes accessed | tf_op | source)
XLA Modules:
  0.0 690.5 jit_solution(5917270509717997618)
XLA Ops:
  7.2 1.7 convert.53
  11.7 15.7 %all-gather = bf16[8,96,13]{1,2,0:T(8,128)(2,1)S(1)} all-gather(bf16[1,96,13]{1,2,0:T(8,128)(2,1)S(1)} %convert_bitcast_fusion), channel_id=1, replica_groups=mesh['dp'=4,'grp'=8] {'grp'}, dimensions={0}, use_global_device_ids=true | all-gather | bytes 22464 | tf_op jit(solution)/shard_map/all_gather | solution.py:335
  30.2 24.3 %all-gather.5.cloned.1.call-done = bf16[768,2304]{1,0:T(8,128)(2,1)} async-done(((bf16[96,2304]{1,0:T(8,128)(2,1)}), bf16[768,2304]{1,0:T(8,128)(2,1)}) %all-gather.5.cloned.1.call-update) | async-done | bytes 3538960 | tf_op jit(solution)/shard_map/all_gather | solution.py:333
  54.5 4.2 fusion.6
  59.9 1.6 copy.103
  61.5 2.5 copy.104
  64.0 1.9 slice.213
  66.8 1.6 copy.101
  68.4 1.4 slice.350
  69.8 1.2 subtract_convert_fusion
  71.0 1.1 pad_maximum_fusion.3
  79.1 3.8 all-to-all-start
  83.1 42.5 %all-gather.9.cloned.1.call-done = bf16[768,3072]{1,0:T(8,128)(2,1)} async-done(((bf16[96,3072]{1,0:T(8,128)(2,1)}), bf16[768,3072]{1,0:T(8,128)(2,1)}) %all-gather.9.cloned.1.call-update) | async-done | bytes 4718608 | tf_op jit(solution)/shard_map/all_gather | solution.py:333
  125.5 6.8 multiply_convert_fusion
  132.4 1.6 copy-done.36
  134.0 4.4 convolution_convert_fusion.1
  138.4 78.0 %all-gather.7.cloned.1.call-done = bf16[3840,768]{1,0:T(8,128)(2,1)} async-done(((bf16[480,768]{1,0:T(8,128)(2,1)}), bf16[3840,768]{1,0:T(8,128)(2,1)}) %all-gather.7.cloned.1.call-update) | async-done | bytes 5898256 | tf_op jit(solution)/shard_map/all_gather | solution.py:333
  216.4 3.2 convolution_convert_fusion.4
  219.6 2.9 reshape_reshape.11
  222.5 1.1 slice.230
  223.6 1.1 slice.285
  225.7 42.0 %shard_map.211 = (f32[8,64,512]{2,1,0:T(8,128)S(1)}, f32[8,64,256]{2,1,0:T(8,128)S(1)}, f32[8,1,512]{2,1,0:T(1,128)S(1)}, f32[8,1,256]{2,1,0:T(1,128)S(1)}) custom-call(s32[8]{0:T(128)S(1)} %bitcast.94, s32[8]{0:T(128)S(1)} %select_reduce_fusion.place_of, s32[1]{0:T(128)} %bitcast.1.half, bf16[8,352,512]{2,1,0:T(8,128)(2,1)S(1)} %all-to-all-done.x_ref), custom_call_target="tpu_custom_call" | custom-call | flops 14495514624 | bytes 5767168 | tf_op jit(solution)/shard_map/pallas_call | solution.py:287
  269.7 3.5 all-to-all-start.1
  273.3 7.2 %convert_reduce_fusion = (f32[3072]{0:T(1024)S(1)}, bf16[512,3072]{1,0:T(8,128)(2,1)S(1)}) fusion(f32[512,3072]{1,0:T(8,128)} %get-tuple-element.111, f32[3072]{0:T(1024)S(1)} %add.210, bf16[512,768]{1,0:T(8,128)(2,1)S(1)} %copy-done.20, bf16[3840,768]{1,0:T(8,128)(2,1)} %all-gather.7.cloned.1.call-done), kind=kOutput, calls=%fused_computation.7 | convolution fusion | flops 2436363264 | bytes 14966784 | tf_op jit(solution)/shard_map/dot_general | solution.py:415
  280.5 1.6 copy-done.38
  282.1 4.8 convolution_convert_fusion.2
  286.9 7.2 %all-to-all-done.1 = bf16[8,96,512]{2,1,0:T(8,128)(2,1)S(1)} async-done(((bf16[8,96,512]{2,1,0:T(8,128)(2,1)}), bf16[8,96,512]{2,1,0:T(8,128)(2,1)S(1)}, u32[]{:S(2)}, u32[]{:S(2)}) %all-to-all-start.1) | async-done | bytes 786464 | tf_op jit(solution)/shard_map/all_to_all | solution.py:281
  294.2 3.5 all-to-all-start.2
  300.4 5.2 pad_maximum_fusion
  305.7 12.9 %all-to-all-done.2.g_ref = bf16[8,96,512]{2,1,0:T(8,128)(2,1)S(1)} async-done(((bf16[8,96,512]{2,1,0:T(8,128)(2,1)}), bf16[8,96,512]{2,1,0:T(8,128)(2,1)S(1)}, u32[]{:S(2)}, u32[]{:S(2)}) %all-to-all-start.2) | async-done | bytes 786464 | tf_op jit(solution)/shard_map/all_to_all | solution.py:281
  319.9 53.3 %shard_map.212 = bf16[8,352,512]{2,1,0:T(8,128)(2,1)} custom-call(s32[8]{0:T(128)S(1)} %bitcast.95, s32[8]{0:T(128)S(1)} %select_reduce_fusion.place_of, s32[1]{0:T(128)} %bitcast.1.half, bf16[8,352,512]{2,1,0:T(8,128)(2,1)} %copy-done, bf16[8,96,512]{2,1,0:T(8,128)(2,1)S(1)} %all-to-all-done.2.g_ref, f32[8,64,512]{2,1,0:T(8,128)S(1)} %copy-done.2, ...), custom_call_target="tpu_custom_call" | custom-call | flops 36238786560 | bytes 8650752 | tf_op jit(solution)/shard_map/pallas_call | solution.py:287
  373.2 3.8 all-to-all-start.3
  377.1 108.6 %all-to-all-done.3 = bf16[8,352,512]{2,1,0:T(8,128)(2,1)S(1)} async-done(((bf16[8,352,512]{2,1,0:T(8,128)(2,1)}), bf16[8,352,512]{2,1,0:T(8,128)(2,1)S(1)}, u32[]{:S(2)}, u32[]{:S(2)}) %all-to-all-start.3) | async-done | bytes 2883616 | tf_op jit(solution)/shard_map/all_to_all | solution.py:281
  489.2 4.1 convolution_convert_fusion
  493.6 7.2 %fusion.65 = f32[512,768]{1,0:T(8,128)} fusion(bf16[512,3072]{1,0:T(8,128)(2,1)} %copy-done.38, bf16[768,3072]{1,0:T(8,128)(2,1)} %all-gather.9.cloned.1.call-done), kind=kOutput, calls=%fused_computation.151 | convolution fusion | flops 2415919104 | bytes 9437184 | tf_op jit(solution)/shard_map/dot_general | solution.py:469
  500.9 6.1 fusion.8
  507.1 4.0 fusion.39
  511.0 4.0 fusion.33
  515.0 28.5 %reduce-scatter.4.cloned.1.call-done = bf16[96,2304]{1,0:T(8,128)(2,1)} async-done(((bf16[768,2304]{1,0:T(8,128)(2,1)}), bf16[96,2304]{1,0:T(8,128)(2,1)}) %reduce-scatter.4.cloned.1.call-update) | async-done | bytes 442384 | tf_op jit(solution)/shard_map/reduce_scatter | solution.py:420
  543.5 58.9 %all-reduce.6.cloned.1.call-done = (bf16[96,3072]{1,0:T(8,128)(2,1)}, bf16[480,768]{1,0:T(8,128)(2,1)}) async-done(((bf16[96,3072]{1,0:T(8,128)(2,1)}, bf16[480,768]{1,0:T(8,128)(2,1)}), (bf16[96,3072]{1,0:T(8,128)(2,1)}, bf16[480,768]{1,0:T(8,128)(2,1)})) %all-reduce.6.cloned.1.call-update) | async-done | bytes 1327120 | tf_op jit(solution)/shard_map/psum | solution.py:440
  602.4 3.5 convert_reduce_fusion.3
  606.2 39.9 %psum.39 = f32[13,768]{1,0:T(8,128)S(1)} all-reduce(f32[13,768]{1,0:T(8,128)S(1)} %concatenate.100), channel_id=1, replica_groups=mesh['dp'=4,'grp'=8] {'dp','grp'}, use_global_device_ids=true, to_apply=%region_27.28 | all-reduce | flops 9984 | bytes 79872 | tf_op jit(solution)/shard_map/psum | solution.py:514
  648.7 1.9 all-reduce.4.cloned.1.call-done
  650.5 1.8 multiply_reduce_fusion.3
  654.3 1.2 convert_element_type.126
  655.5 16.8 %psum.38 = f32[]{:T(128)} all-reduce(f32[]{:T(128)S(6)} %add.227), channel_id=1, replica_groups=mesh['dp'=4,'grp'=8] {'grp'}, use_global_device_ids=true, to_apply=%region_19.20 | all-reduce | flops 1 | bytes 8 | tf_op jit(solution)/shard_map/psum | solution.py:515
  673.7 4.4 multiply_subtract_fusion.1
  679.0 3.1 multiply_subtract_fusion
  (186 shorter events, 28.2 us)
Async XLA Ops:
  7.2 47.4 %all-gather.5.cloned.1.call-start = ((), (), s32[]{:S(2)}) async-start(), calls=%async_computation.7 | async-start | bytes 3981312 | tf_op jit(solution)/shard_map/all_gather | solution.py:333
  8.9 1.8 copy-start.8
  9.7 115.8 %all-gather.9.cloned.1.call-start = ((), (), s32[]{:S(2)}) async-start(), calls=%async_computation.9 | async-start | bytes 5308416 | tf_op jit(solution)/shard_map/all_gather | solution.py:333
  10.7 1.1 copy-start.25
  10.7 16.9 %copy-start.3 = (s32[1,8]{1,0:T(1,128)S(1)}, s32[1,8]{1,0:T(1,128)}, u32[]{:S(2)}) copy-start(s32[1,8]{1,0:T(1,128)} %param.14) | copy-start | bytes 100
  10.7 19.0 %copy-start.5 = (bf16[512,768]{1,0:T(8,128)(2,1)S(1)}, bf16[512,768]{1,0:T(8,128)(2,1)}, u32[]{:S(2)}) copy-start(bf16[512,768]{1,0:T(8,128)(2,1)} %param.12) | copy-start | bytes 2359300
  10.7 205.7 %all-gather.7.cloned.1.call-start = ((), (), s32[]{:S(2)}) async-start(), calls=%async_computation.8 | async-start | bytes 6635520 | tf_op jit(solution)/shard_map/all_gather | solution.py:333
  29.0 40.8 %copy-start.21 = (f32[8,512]{1,0:T(8,128)}, f32[8,512]{1,0:T(8,128)S(1)}, u32[]{:S(2)}) copy-start(f32[8,512]{1,0:T(8,128)S(1)} %get-tuple-element.25) | copy-start | bytes 49156
  29.0 40.7 %copy-start.23 = (f32[8,512]{1,0:T(8,128)}, f32[8,512]{1,0:T(8,128)S(1)}, u32[]{:S(2)}) copy-start(f32[8,512]{1,0:T(8,128)S(1)} %get-tuple-element.26) | copy-start | bytes 49156
  29.7 29.0 %copy-start.27 = (f32[768]{0:T(1024)}, f32[768]{0:T(1024)S(1)}, u32[]{:S(2)}) copy-start(f32[768]{0:T(1024)S(1)} %get-tuple-element.57) | copy-start | bytes 9220
  29.7 29.0 %copy-start.33 = (f32[768]{0:T(1024)}, f32[768]{0:T(1024)S(1)}, u32[]{:S(2)}) copy-start(f32[768]{0:T(1024)S(1)} %get-tuple-element.56) | copy-start | bytes 9220
  61.5 4.4 copy-start.10
  73.9 2.5 copy-start.13
  79.1 146.6 %all-to-all-start = ((bf16[8,352,512]{2,1,0:T(8,128)(2,1)}), bf16[8,352,512]{2,1,0:T(8,128)(2,1)S(1)}, u32[]{:S(2)}, u32[]{:S(2)}) async-start(bf16[8,352,512]{2,1,0:T(8,128)(2,1)} %constant_dynamic-update-slice_fusion), calls=%async_computation | async-start | bytes 5767168 | tf_op jit(solution)/shard_map/all_to_all | solution.py:281
  125.5 8.5 %copy-start.19 = (bf16[512,768]{1,0:T(8,128)(2,1)S(1)}, bf16[512,768]{1,0:T(8,128)(2,1)}, u32[]{:S(2)}) copy-start(bf16[512,768]{1,0:T(8,128)(2,1)} %param.13) | copy-start | bytes 2359300
  132.4 1.6 copy-start.36
  225.7 42.0 %copy-start = (bf16[8,352,512]{2,1,0:T(8,128)(2,1)}, bf16[8,352,512]{2,1,0:T(8,128)(2,1)S(1)}, u32[]{:S(2)}) copy-start(bf16[8,352,512]{2,1,0:T(8,128)(2,1)S(1)} %all-to-all-done.x_ref) | copy-start | bytes 8650756
  268.7 4.6 copy-start.20
  269.7 24.5 %all-to-all-start.1 = ((bf16[8,96,512]{2,1,0:T(8,128)(2,1)}), bf16[8,96,512]{2,1,0:T(8,128)(2,1)S(1)}, u32[]{:S(2)}, u32[]{:S(2)}) async-start(bf16[8,96,512]{2,1,0:T(8,128)(2,1)} %maximum_maximum_fusion), calls=%async_computation.1 | async-start | bytes 1572864 | tf_op jit(solution)/shard_map/all_to_all | solution.py:281
  273.3 8.8 %copy-start.6 = (bf16[512,768]{1,0:T(8,128)(2,1)S(1)}, bf16[512,768]{1,0:T(8,128)(2,1)}, u32[]{:S(2)}) copy-start(bf16[512,768]{1,0:T(8,128)(2,1)} %param.12) | copy-start | bytes 2359300
  280.5 1.6 copy-start.38
  294.2 24.5 %all-to-all-start.2 = ((bf16[8,96,512]{2,1,0:T(8,128)(2,1)}), bf16[8,96,512]{2,1,0:T(8,128)(2,1)S(1)}, u32[]{:S(2)}, u32[]{:S(2)}) async-start(bf16[8,96,512]{2,1,0:T(8,128)(2,1)} %maximum_maximum_fusion.1), calls=%async_computation.2 | async-start | bytes 1572864 | tf_op jit(solution)/shard_map/all_to_all | solution.py:281
  297.7 209.2 %reduce-scatter.6.cloned.1.call-start = ((), (), s32[]{:S(2)}) async-start(), calls=%async_computation.11 | async-start | bytes 5308416 | tf_op jit(solution)/shard_map/reduce_scatter | solution.py:420
  318.6 1.2 copy-start.2
  318.7 188.3 %reduce-scatter.8.cloned.1.call-start = ((), (), s32[]{:S(2)}) async-start(), calls=%async_computation.12 | async-start | bytes 6635520 | tf_op jit(solution)/shard_map/reduce_scatter | solution.py:420
  373.2 3.8 copy-start.24
  373.2 112.4 %all-to-all-start.3 = ((bf16[8,352,512]{2,1,0:T(8,128)(2,1)}), bf16[8,352,512]{2,1,0:T(8,128)(2,1)S(1)}, u32[]{:S(2)}, u32[]{:S(2)}) async-start(bf16[8,352,512]{2,1,0:T(8,128)(2,1)} %shard_map.212), calls=%async_computation.3 | async-start | bytes 5767168 | tf_op jit(solution)/shard_map/all_to_all | solution.py:281
  377.0 166.5 %reduce-scatter.4.cloned.1.call-start = ((), (), s32[]{:S(2)}) async-start(), calls=%async_computation.10 | async-start | bytes 3981312 | tf_op jit(solution)/shard_map/reduce_scatter | solution.py:420
  488.0 1.2 copy-start.7
  488.0 1.2 copy-start.28
  488.0 1.1 copy-start.34
  493.3 109.1 %all-reduce.6.cloned.1.call-start = ((), (), s32[]{:S(2)}) async-start(), calls=%async_computation.14 | async-start | bytes 2654208 | tf_op jit(solution)/shard_map/psum | solution.py:440
  493.6 7.2 %copy-start.37 = (bf16[512,3072]{1,0:T(8,128)(2,1)S(1)}, bf16[512,3072]{1,0:T(8,128)(2,1)}, u32[]{:S(2)}) copy-start(bf16[512,3072]{1,0:T(8,128)(2,1)} %copy-done.36) | copy-start | bytes 9437188
  500.9 6.2 copy-start.31
  500.9 6.2 copy-start.32
  507.0 143.6 %all-reduce.4.cloned.1.call-start = ((), (), s32[]{:S(2)}) async-start(), calls=%async_computation.13 | async-start | bytes 884736 | tf_op jit(solution)/shard_map/psum | solution.py:499
  507.1 4.0 copy-start.17
  507.1 4.0 copy-start.35
  602.4 44.4 %copy-start.12 = (bf16[96,3072]{1,0:T(8,128)(2,1)S(1)}, bf16[96,3072]{1,0:T(8,128)(2,1)}, u32[]{:S(2)}) copy-start(bf16[96,3072]{1,0:T(8,128)(2,1)} %get-tuple-element.36) | copy-start | bytes 1769476
  602.4 45.3 %copy-start.11 = (bf16[480,768]{1,0:T(8,128)(2,1)S(1)}, bf16[480,768]{1,0:T(8,128)(2,1)}, u32[]{:S(2)}) copy-start(bf16[480,768]{1,0:T(8,128)(2,1)} %get-tuple-element.37) | copy-start | bytes 2211844
  605.9 67.7 %copy-start.9 = (f32[480,768]{1,0:T(8,128)S(1)}, f32[480,768]{1,0:T(8,128)}, u32[]{:S(2)}) copy-start(f32[480,768]{1,0:T(8,128)} %param.16) | copy-start | bytes 4423684
  673.7 4.5 copy-start.26
  673.7 4.5 copy-start.29
  673.7 4.5 copy-start.30
  673.7 5.2 copy-start.16
  673.7 5.2 copy-start.4
  673.7 5.2 copy-start.14
  673.7 5.2 copy-start.15
  (3 other events, 2.6 us)
Sparse Core Ops, SparseCore 0:
  10.2 44.2 all-gather.4
  56.8 68.7 all-gather.8
  127.7 88.6 all-gather.6
  318.8 53.8 reduce-scatter.5
  374.8 117.7 reduce-scatter.7
  494.9 48.5 reduce-scatter.3
  546.7 55.6 all-reduce.5
  605.7 44.8 all-reduce.3

commit v2 on v1

--- a/solution.py
+++ b/solution.py
@@ -323,6 +323,7 @@
     width = tokens.shape[1]
     rows_here = tokens.shape[0]
     groups = lax.axis_size("grp")
+    parts = lax.axis_size("dp")
     score_scale = 1.0 / math.sqrt(HEAD)
     contract_rows = (((0,), (0,)), ((), ()))
     contract_last = (((1,), (1,)), ((), ()))
@@ -376,14 +377,6 @@
             axis=1,
         )
     )
-    grad_context = (
-        lax.dot_general(weight_ctx, cotangent, contract_last, preferred_element_type=f32)
-        .astype(bf16)
-        .reshape(HEADS, HEAD, rows_here)
-    )
-    grad_packed = exchange(
-        jnp.concatenate([split_alone(grad_context), split_halves(grad_context)], axis=1)
-    )
     tasks = (order_row, place_of, half)
     pair_work = groups * (groups + 1) * 3 * rows_here * rows_here * HEAD
     stage = (2, groups, rows_here, HEAD)
@@ -404,6 +397,18 @@
     context_back = exchange(
         jnp.concatenate([context_alone, fold_half(context_both)], axis=1).astype(bf16)
     )
+    weight_ctx, weight_ffn, context_both = lax.optimization_barrier(
+        (weight_ctx, weight_ffn, context_both)
+    )
+    grad_context = (
+        lax.dot_general(weight_ctx, cotangent, contract_last, preferred_element_type=f32)
+        .astype(bf16)
+        .reshape(HEADS, HEAD, rows_here)
+    )
+    grad_packed = exchange(
+        jnp.concatenate([split_alone(grad_context), split_halves(grad_context)], axis=1)
+    )
+    weight_feed, context_alone = lax.optimization_barrier((weight_feed, context_alone))
     hidden_pre = (
         lax.dot_general(
             feed_in, weight_feed, (((1,), (0,)), ((), ())), preferred_element_type=f32
@@ -416,8 +421,16 @@
         * gelu_slope(hidden_pre)
     ).astype(bf16)
 
-    def scatter_rows(raw):
-        return lax.psum_scatter(raw, "grp", scatter_dimension=0, tiled=True)
+    def order_rows(raw):
+        rows, columns = raw.shape
+        ordered = raw.reshape(groups, parts, rows // (groups * parts), columns)
+        return ordered.transpose(1, 0, 2, 3).reshape(rows, columns)
+
+    def scatter_rows(ordered):
+        return lax.psum_scatter(ordered, ("dp", "grp"), scatter_dimension=0, tiled=True)
+
+    def join_rows(mine):
+        return lax.all_gather(mine, "dp", axis=0, tiled=True).astype(f32)
 
     def rows_product(left, right):
         return lax.dot_general(left, right, contract_rows, preferred_element_type=f32)
@@ -434,10 +447,9 @@
         axis=0,
     )
     raw_feed, raw_out, packed, grad_packed = lax.optimization_barrier(
-        (raw_feed, raw_out, packed, grad_packed)
-    )
-    mine_feed, mine_out = scatter_rows(raw_feed), scatter_rows(raw_out)
-    sum_feed, sum_out = lax.psum((mine_feed, mine_out), "dp")
+        (order_rows(raw_feed), order_rows(raw_out), packed, grad_packed)
+    )
+    mine_out, mine_feed = scatter_rows(raw_out), scatter_rows(raw_feed)
     grads_back = exchange(
         local_call(
             backward_kernel,
@@ -494,10 +506,10 @@
         .reshape(3 * width, rows_here)
     )
     raw_attn = lax.dot_general(attn_in, grad_proj, flat, preferred_element_type=f32)
-    mine_attn = scatter_rows(raw_attn.astype(bf16))
-    mine_attn, sum_feed, sum_out = lax.optimization_barrier((mine_attn, sum_feed, sum_out))
-    sum_attn = lax.psum(mine_attn, "dp").astype(f32)
-    sum_feed, sum_out = sum_feed.astype(f32), sum_out.astype(f32)
+    raw_attn, mine_out, mine_feed = lax.optimization_barrier(
+        (order_rows(raw_attn.astype(bf16)), mine_out, mine_feed)
+    )
+    mine_attn = scatter_rows(raw_attn)
     back_one = lax.dot_general(grad_proj, weight_attn, flat, preferred_element_type=f32)
     input_one, gain_one, bias_one = norm_backward(back_one, normed_one, inverse_one, vector_rows[0])
     token_grad = (cotangent.astype(f32) + input_one + input_two).astype(bf16)
@@ -512,7 +524,10 @@
         axis=0,
     )
     vector_sum = lax.psum(raw_vec, ("dp", "grp"))
-    matrix_total = lax.psum(square_sum((sum_attn, sum_feed, sum_out)), "grp")
+    sum_feed, sum_out, sum_attn = join_rows(mine_feed), join_rows(mine_out), join_rows(mine_attn)
+    squares = square_sum(tuple(mine.astype(f32) for mine in (mine_attn, mine_feed, mine_out)))
+    squares, vector_sum = lax.optimization_barrier((squares, vector_sum))
+    matrix_total = lax.psum(squares, ("dp", "grp"))
     total = matrix_total + jnp.sum(vector_sum * vector_sum)
     clip_norm = jnp.sqrt(total)
     factor = jnp.minimum(1.0, CLIP_LIMIT / (clip_norm + 1e-06))

time: 697 us -> 720 us (1.033)
  blocking collectives: 72.4 us -> 132 us
  waiting for transfers between devices: 363 us -> 330 us
  local copies, waits for them, and re-layouts: 32.8 us -> 44.3 us
  matrix products: 56.7 us -> 45.4 us
    reduce_scatter x3, waiting for transfers between devices: 28.5 us -> 119 us  [scatter_rows(): lax.psum_scatter(ordered, ('dp', 'grp'), scatter_dimension=0, tiled=True)]
    psum x2 -> x0, waiting for transfers between devices: 60.8 us -> none  [the longest x1 58.9 us: body(): sum_feed, sum_out = lax.psum((mine_feed, mine_out), 'dp')]
    all_gather x3, waiting for transfers between devices: 145 us -> 91.4 us  [gather_rows(): return lax.all_gather(shard.astype(bf16), 'grp', axis=0, tiled=True)]
    all_gather x0 -> x3, blocking collectives: none -> 35.3 us  [join_rows(): return lax.all_gather(mine, 'dp', axis=0, tiled=True).astype(f32)]
    psum x1, blocking collectives: 16.8 us -> 39.9 us  [body(): matrix_total = lax.psum(squares, ('dp', 'grp'))]
    all_to_all x4, waiting for transfers between devices: 129 us -> 119 us  [exchange(): return lax.all_to_all(packed, 'grp', 0, 0, tiled=True)]
    transpose x0 -> x3, local copies, waits for them, and re-layouts: none -> 7.51 us  [order_rows(): return ordered.transpose(1, 0, 2, 3).reshape(rows, columns)]
    slice x0 -> x2, local copies, waits for them, and re-layouts: none -> 7.21 us  [body(): weight_ctx, weight_ffn = (weight_ctx[:width], weight_ctx[width:])]
  transfers between devices with their start and end apart: 12 -> 10, of which waited for: 9 -> 7; matrix products, arithmetic and copies ran while one was open for 15% -> 13% of each run, Pallas kernels for 8% -> 13%
where the time goes in v2:
time: 720 us; the launch traced here: 713 us
  waiting for transfers between devices  330 us (46%)
  blocking collectives  132 us (18%)
  Pallas kernels  95.1 us (13%)
  matrix products  45.4 us (6%)
  local copies, waits for them, and re-layouts  44.3 us (6%)
  other arithmetic  28.6 us (4%)
  between operations  20.6 us (3%)
  starting transfers between devices  16.8 us (2%)
    reduce_scatter x3, waiting for transfers between devices, scatter_rows(): lax.psum_scatter(ordered, ('dp', 'grp'), scatter_dimension=0, tiled=True)  119 us
    all_to_all x4, waiting for transfers between devices, exchange(): return lax.all_to_all(packed, 'grp', 0, 0, tiled=True)  119 us
    pallas_call x2, Pallas kernels, local_call(): pl.pallas_call(kernel, out_shape=outputs, in_specs=[smem] * 3 + [vmem] *...  95.1 us
    all_gather x3, waiting for transfers between devices, gather_rows(): return lax.all_gather(shard.astype(bf16), 'grp', axis=0, tiled=True)  91.4 us
    psum x1, blocking collectives, body(): vector_sum = lax.psum(raw_vec, ('dp', 'grp'))  40.9 us
    psum x1, blocking collectives, body(): matrix_total = lax.psum(squares, ('dp', 'grp'))  39.9 us
    all_gather x3, blocking collectives, join_rows(): return lax.all_gather(mine, 'dp', axis=0, tiled=True).astype(f32)  35.3 us
    all_to_all x4, starting transfers between devices, exchange(): return lax.all_to_all(packed, 'grp', 0, 0, tiled=True)  16.4 us
  transfers between devices with their start and end apart: 10, of which 7 were waited for; matrix products, arithmetic and copies ran while one was open for 13% of the time, Pallas kernels for 13%

profile of v2, /device:TPU:0, one launch (start us, length us, event | category | flops | bytes accessed | tf_op | source)
XLA Modules:
  0.0 712.6 jit_solution(1654478712637926977)
XLA Ops:
  7.2 1.8 convert.54
  11.9 15.7 %all-gather = bf16[8,96,13]{1,2,0:T(8,128)(2,1)S(1)} all-gather(bf16[1,96,13]{1,2,0:T(8,128)(2,1)S(1)} %convert_bitcast_fusion), channel_id=1, replica_groups=mesh['dp'=4,'grp'=8] {'grp'}, dimensions={0}, use_global_device_ids=true | all-gather | bytes 22464 | tf_op jit(solution)/shard_map/all_gather | solution.py:336
  30.4 24.2 %all-gather.5.cloned.1.call-done = bf16[768,2304]{1,0:T(8,128)(2,1)} async-done(((bf16[96,2304]{1,0:T(8,128)(2,1)}), bf16[768,2304]{1,0:T(8,128)(2,1)}) %all-gather.5.cloned.1.call-update) | async-done | bytes 3538960 | tf_op jit(solution)/shard_map/all_gather | solution.py:334
  54.6 4.2 fusion.6
  58.8 2.2 copy-done.13
  61.2 1.6 copy.116
  62.8 1.6 copy.118
  64.5 1.9 subtract_convert_fusion
  66.5 1.4 slice.341
  67.8 1.5 slice.340
  76.5 3.6 all-to-all-start
  80.3 67.2 %all-gather.7.cloned.1.call-done = bf16[3840,768]{1,0:T(8,128)(2,1)} async-done(((bf16[480,768]{1,0:T(8,128)(2,1)}), bf16[3840,768]{1,0:T(8,128)(2,1)}) %all-gather.7.cloned.1.call-update) | async-done | bytes 5898256 | tf_op jit(solution)/shard_map/all_gather | solution.py:334
  147.5 2.4 slice.277
  149.8 4.9 slice.278
  154.7 24.9 %all-to-all-done.x_ref = bf16[8,352,512]{2,1,0:T(8,128)(2,1)S(1)} async-done(((bf16[8,352,512]{2,1,0:T(8,128)(2,1)}), bf16[8,352,512]{2,1,0:T(8,128)(2,1)S(1)}, u32[]{:S(2)}, u32[]{:S(2)}) %all-to-all-start) | async-done | bytes 2883616 | tf_op jit(solution)/shard_map/all_to_all | solution.py:281
  179.6 42.0 %shard_map.211 = (f32[8,64,512]{2,1,0:T(8,128)S(1)}, f32[8,64,256]{2,1,0:T(8,128)S(1)}, f32[8,1,512]{2,1,0:T(1,128)S(1)}, f32[8,1,256]{2,1,0:T(1,128)S(1)}) custom-call(s32[8]{0:T(128)S(1)} %bitcast.112, s32[8]{0:T(128)S(1)} %select_reduce_fusion.place_of, s32[1]{0:T(128)} %bitcast.1.half, bf16[8,352,512]{2,1,0:T(8,128)(2,1)S(1)} %all-to-all-done.x_ref), custom_call_target="tpu_custom_call" | custom-call | flops 14495514624 | bytes 5767168 | tf_op jit(solution)/shard_map/pallas_call | solution.py:287
  223.7 4.1 all-to-all-start.1
  227.8 6.4 multiply_convert_fusion
  234.2 6.2 convert_reduce_fusion
  240.4 3.3 convolution_convert_fusion.2
  243.7 2.5 copy.124
  248.5 1.2 copy-done.47
  249.7 4.3 convolution_convert_fusion.1
  254.0 5.1 all-to-all-start.2
  263.1 2.9 copy.125
  266.1 14.0 %all-to-all-done.2.g_ref = bf16[8,96,512]{2,1,0:T(8,128)(2,1)S(1)} async-done(((bf16[8,96,512]{2,1,0:T(8,128)(2,1)}), bf16[8,96,512]{2,1,0:T(8,128)(2,1)S(1)}, u32[]{:S(2)}, u32[]{:S(2)}) %all-to-all-start.2) | async-done | bytes 786464 | tf_op jit(solution)/shard_map/all_to_all | solution.py:281
  280.1 1.2 copy-done.2
  281.3 53.1 %shard_map.212 = bf16[8,352,512]{2,1,0:T(8,128)(2,1)} custom-call(s32[8]{0:T(128)S(1)} %bitcast.113, s32[8]{0:T(128)S(1)} %select_reduce_fusion.place_of, s32[1]{0:T(128)} %bitcast.1.half, bf16[8,352,512]{2,1,0:T(8,128)(2,1)} %copy-done, bf16[8,96,512]{2,1,0:T(8,128)(2,1)S(1)} %all-to-all-done.2.g_ref, f32[8,64,512]{2,1,0:T(8,128)S(1)} %copy-done.2, ...), custom_call_target="tpu_custom_call" | custom-call | flops 36238786560 | bytes 8650752 | tf_op jit(solution)/shard_map/pallas_call | solution.py:287
  334.4 3.6 all-to-all-start.3
  338.7 80.1 %all-to-all-done.3 = bf16[8,352,512]{2,1,0:T(8,128)(2,1)S(1)} async-done(((bf16[8,352,512]{2,1,0:T(8,128)(2,1)}), bf16[8,352,512]{2,1,0:T(8,128)(2,1)S(1)}, u32[]{:S(2)}, u32[]{:S(2)}) %all-to-all-start.3) | async-done | bytes 2883616 | tf_op jit(solution)/shard_map/all_to_all | solution.py:281
  425.1 1.1 multiply_subtract_fusion.3
  427.4 2.3 convolution_convert_fusion
  429.7 2.1 copy.131
  431.8 97.1 %reduce-scatter.4.cloned.1.call-done = bf16[120,768]{1,0:T(8,128)(2,1)} async-done(((bf16[3840,768]{1,0:T(8,128)(2,1)}), bf16[120,768]{1,0:T(8,128)(2,1)}) %reduce-scatter.4.cloned.1.call-update) | async-done | bytes 184336 | tf_op jit(solution)/shard_map/reduce_scatter | solution.py:430
  528.9 6.0 fusion.59
  535.0 5.2 fusion.60
  540.3 1.8 fusion.36
  543.2 4.1 fusion.30
  547.4 3.5 convert_reduce_fusion.3
  551.1 40.9 %psum.14 = f32[13,768]{1,0:T(8,128)S(1)} all-reduce(f32[13,768]{1,0:T(8,128)S(1)} %concatenate.103), channel_id=1, replica_groups=mesh['dp'=4,'grp'=8] {'dp','grp'}, use_global_device_ids=true, to_apply=%region_23.24 | all-reduce | flops 9984 | bytes 79872 | tf_op jit(solution)/shard_map/psum | solution.py:526
  592.0 11.4 %all_gather.26 = bf16[96,3072]{1,0:T(8,128)(2,1)S(1)} all-gather(bf16[24,3072]{1,0:T(8,128)(2,1)S(1)} %copy-done.28), channel_id=1, replica_groups=mesh['dp'=4,'grp'=8] {'dp'}, dimensions={0}, use_global_device_ids=true | all-gather | bytes 737280 | tf_op jit(solution)/shard_map/all_gather | solution.py:433
  604.7 12.5 %all_gather.27 = bf16[480,768]{1,0:T(8,128)(2,1)S(1)} all-gather(bf16[120,768]{1,0:T(8,128)(2,1)S(1)} %copy-done.27), channel_id=1, replica_groups=mesh['dp'=4,'grp'=8] {'dp'}, dimensions={0}, use_global_device_ids=true | all-gather | bytes 921600 | tf_op jit(solution)/shard_map/all_gather | solution.py:433
  617.3 22.1 %reduce-scatter.8.cloned.1.call-done = bf16[24,2304]{1,0:T(8,128)(2,1)} async-done(((bf16[768,2304]{1,0:T(8,128)(2,1)}), bf16[24,2304]{1,0:T(8,128)(2,1)}) %reduce-scatter.8.cloned.1.call-update) | async-done | bytes 110608 | tf_op jit(solution)/shard_map/reduce_scatter | solution.py:430
  639.4 1.6 multiply_reduce_fusion.4
  642.9 39.9 %psum.15 = f32[]{:T(128)} all-reduce(f32[]{:T(128)S(6)} %add.221), channel_id=1, replica_groups=mesh['dp'=4,'grp'=8] {'dp','grp'}, use_global_device_ids=true, to_apply=%region_24.25 | all-reduce | flops 1 | bytes 8 | tf_op jit(solution)/shard_map/psum | solution.py:530
  684.8 4.4 multiply_subtract_fusion.1
  689.9 11.3 %all_gather.25 = bf16[96,2304]{1,0:T(8,128)(2,1)S(1)} all-gather(bf16[24,2304]{1,0:T(8,128)(2,1)S(1)} %copy-done.29), channel_id=1, replica_groups=mesh['dp'=4,'grp'=8] {'dp'}, dimensions={0}, use_global_device_ids=true | all-gather | bytes 552960 | tf_op jit(solution)/shard_map/all_gather | solution.py:433
  701.3 3.1 multiply_subtract_fusion
  (208 shorter events, 32.8 us)
Async XLA Ops:
  7.2 2.7 copy-start.8
  7.2 47.4 %all-gather.5.cloned.1.call-start = ((), (), s32[]{:S(2)}) async-start(), calls=%async_computation.7 | async-start | bytes 3981312 | tf_op jit(solution)/shard_map/all_gather | solution.py:334
  9.8 2.0 copy-start.36
  9.9 18.5 %copy-start.5 = (bf16[512,768]{1,0:T(8,128)(2,1)S(1)}, bf16[512,768]{1,0:T(8,128)(2,1)}, u32[]{:S(2)}) copy-start(bf16[512,768]{1,0:T(8,128)(2,1)} %param.12) | copy-start | bytes 2359300
  9.9 137.6 %all-gather.7.cloned.1.call-start = ((), (), s32[]{:S(2)}) async-start(), calls=%async_computation.8 | async-start | bytes 6635520 | tf_op jit(solution)/shard_map/all_gather | solution.py:334
  10.9 18.0 %copy-start.3 = (s32[1,8]{1,0:T(1,128)S(1)}, s32[1,8]{1,0:T(1,128)}, u32[]{:S(2)}) copy-start(s32[1,8]{1,0:T(1,128)} %param.14) | copy-start | bytes 100
  10.9 211.8 %all-gather.9.cloned.1.call-start = ((), (), s32[]{:S(2)}) async-start(), calls=%async_computation.9 | async-start | bytes 5308416 | tf_op jit(solution)/shard_map/all_gather | solution.py:334
  28.3 30.5 %copy-start.38 = (f32[768]{0:T(1024)}, f32[768]{0:T(1024)S(1)}, u32[]{:S(2)}) copy-start(f32[768]{0:T(1024)S(1)} %get-tuple-element.71) | copy-start | bytes 9220
  28.3 30.5 %copy-start.44 = (f32[768]{0:T(1024)}, f32[768]{0:T(1024)S(1)}, u32[]{:S(2)}) copy-start(f32[768]{0:T(1024)S(1)} %get-tuple-element.70) | copy-start | bytes 9220
  30.3 34.1 %copy-start.32 = (f32[8,512]{1,0:T(8,128)}, f32[8,512]{1,0:T(8,128)S(1)}, u32[]{:S(2)}) copy-start(f32[8,512]{1,0:T(8,128)S(1)} %get-tuple-element.32) | copy-start | bytes 49156
  30.4 34.1 %copy-start.34 = (f32[8,512]{1,0:T(8,128)}, f32[8,512]{1,0:T(8,128)S(1)}, u32[]{:S(2)}) copy-start(f32[8,512]{1,0:T(8,128)S(1)} %get-tuple-element.33) | copy-start | bytes 49156
  58.8 2.2 copy-start.13
  62.8 1.7 copy-start.12
  69.5 1.4 copy-start.30
  69.6 1.4 copy-start.31
  76.5 103.1 %all-to-all-start = ((bf16[8,352,512]{2,1,0:T(8,128)(2,1)}), bf16[8,352,512]{2,1,0:T(8,128)(2,1)S(1)}, u32[]{:S(2)}, u32[]{:S(2)}) async-start(bf16[8,352,512]{2,1,0:T(8,128)(2,1)} %constant_dynamic-update-slice_fusion), calls=%async_computation | async-start | bytes 5767168 | tf_op jit(solution)/shard_map/all_to_all | solution.py:281
  179.6 42.0 %copy-start = (bf16[8,352,512]{2,1,0:T(8,128)(2,1)}, bf16[8,352,512]{2,1,0:T(8,128)(2,1)S(1)}, u32[]{:S(2)}) copy-start(bf16[8,352,512]{2,1,0:T(8,128)(2,1)S(1)} %all-to-all-done.x_ref) | copy-start | bytes 8650756
  222.7 5.1 copy-start.6
  223.7 30.3 %all-to-all-start.1 = ((bf16[8,96,512]{2,1,0:T(8,128)(2,1)}), bf16[8,96,512]{2,1,0:T(8,128)(2,1)S(1)}, u32[]{:S(2)}, u32[]{:S(2)}) async-start(bf16[8,96,512]{2,1,0:T(8,128)(2,1)} %maximum_maximum_fusion), calls=%async_computation.1 | async-start | bytes 1572864 | tf_op jit(solution)/shard_map/all_to_all | solution.py:281
  227.8 6.4 copy-start.24
  240.4 3.3 copy-start.48
  243.7 2.5 copy-start.18
  247.3 2.4 copy-start.47
  254.0 26.0 %all-to-all-start.2 = ((bf16[8,96,512]{2,1,0:T(8,128)(2,1)}), bf16[8,96,512]{2,1,0:T(8,128)(2,1)S(1)}, u32[]{:S(2)}, u32[]{:S(2)}) async-start(bf16[8,96,512]{2,1,0:T(8,128)(2,1)} %maximum_maximum_fusion.1), calls=%async_computation.2 | async-start | bytes 1572864 | tf_op jit(solution)/shard_map/all_to_all | solution.py:281
  259.1 172.7 %reduce-scatter.6.cloned.1.call-start = ((), (), s32[]{:S(2)}) async-start(), calls=%async_computation.11 | async-start | bytes 4866048 | tf_op jit(solution)/shard_map/reduce_scatter | solution.py:430
  260.0 2.8 copy-start.10
  260.0 3.1 copy-start.22
  334.4 84.5 %all-to-all-start.3 = ((bf16[8,352,512]{2,1,0:T(8,128)(2,1)}), bf16[8,352,512]{2,1,0:T(8,128)(2,1)S(1)}, u32[]{:S(2)}, u32[]{:S(2)}) async-start(bf16[8,352,512]{2,1,0:T(8,128)(2,1)} %shard_map.212), calls=%async_computation.3 | async-start | bytes 5767168 | tf_op jit(solution)/shard_map/all_to_all | solution.py:281
  338.0 190.9 %reduce-scatter.4.cloned.1.call-start = ((), (), s32[]{:S(2)}) async-start(), calls=%async_computation.10 | async-start | bytes 6082560 | tf_op jit(solution)/shard_map/reduce_scatter | solution.py:430
  338.6 300.8 %reduce-scatter.8.cloned.1.call-start = ((), (), s32[]{:S(2)}) async-start(), calls=%async_computation.12 | async-start | bytes 3649536 | tf_op jit(solution)/shard_map/reduce_scatter | solution.py:430
  424.2 2.0 copy-start.14
  528.9 6.1 copy-start.49
  535.0 5.2 copy-start.19
  535.0 5.2 copy-start.23
  535.0 5.2 copy-start.42
  535.0 5.2 copy-start.43
  540.2 1.9 copy-start.17
  540.3 2.9 copy-start.46
  547.4 44.6 %copy-start.28 = (bf16[24,3072]{1,0:T(8,128)(2,1)S(1)}, bf16[24,3072]{1,0:T(8,128)(2,1)}, u32[]{:S(2)}) copy-start(bf16[24,3072]{1,0:T(8,128)(2,1)} %reduce-scatter.6.cloned.1.call-done) | copy-start | bytes 442372
  547.4 56.7 %copy-start.27 = (bf16[120,768]{1,0:T(8,128)(2,1)S(1)}, bf16[120,768]{1,0:T(8,128)(2,1)}, u32[]{:S(2)}) copy-start(bf16[120,768]{1,0:T(8,128)(2,1)} %reduce-scatter.4.cloned.1.call-done) | copy-start | bytes 552964
  550.9 133.8 %copy-start.9 = (f32[480,768]{1,0:T(8,128)S(1)}, f32[480,768]{1,0:T(8,128)}, u32[]{:S(2)}) copy-start(f32[480,768]{1,0:T(8,128)} %param.16) | copy-start | bytes 4423684
  684.8 4.5 copy-start.37
  684.8 4.5 copy-start.40
  684.8 4.4 copy-start.41
  684.8 5.1 copy-start.29
  684.8 16.5 %copy-start.4 = (f32[96,5376]{1,0:T(8,128)S(1)}, f32[96,5376]{1,0:T(8,128)}, u32[]{:S(2)}) copy-start(f32[96,5376]{1,0:T(8,128)} %param.15) | copy-start | bytes 6193156
  684.8 16.5 %copy-start.15 = (f32[96,5376]{1,0:T(8,128)S(1)}, f32[96,5376]{1,0:T(8,128)}, u32[]{:S(2)}) copy-start(f32[96,5376]{1,0:T(8,128)} %param.18) | copy-start | bytes 6193156
  684.8 16.5 %copy-start.16 = (f32[96,5376]{1,0:T(8,128)S(1)}, f32[96,5376]{1,0:T(8,128)}, u32[]{:S(2)}) copy-start(f32[96,5376]{1,0:T(8,128)} %param.21) | copy-start | bytes 6193156
  (12 other events, 12.9 us)
Sparse Core Ops, SparseCore 0:
  10.2 44.2 all-gather.4
  56.8 90.6 all-gather.6
  149.7 67.4 all-gather.8
  280.2 130.9 reduce-scatter.5
  417.6 111.2 reduce-scatter.3
  535.1 104.2 reduce-scatter.7
